TPU v7x, 32 devices: a whole 2x2x4 slice. The times are simulated.
32 devices in a mesh: section: 2 (over x), dp: 16 (over z, y, core).
Axes of the slice: x: 2, y: 2, z: 4, core: 2. Of those that a mesh axis runs over, the one named last changes fastest.
Arguments:
- block_in: bfloat16 [2, 32, 256, 768], P('section', 'dp'), may hold values from -6 to 6
- cotangent: bfloat16 [32, 256, 768], P('dp'), may hold values from -6 to 6
- lengths: int32 [32], P('dp'), may hold values from 63 to 256, as said below
- sources: int32 [32], P('dp'), may hold values from 0 to 2
- loss_weight: int32 [3], replicated, may hold values from 1 to 3
- gains: bfloat16 [2, 3, 768], P('section', None, 'dp'), may hold values from 0.5 to 1.5
- qkv_weight: bfloat16 [2, 768, 2304], P('section', 'dp'), may hold values from -0.21875 to 0.21875
- out_weight: bfloat16 [2, 768, 768], P('section', 'dp'), may hold values from -2.5 to 2.5
- cross_weight: bfloat16 [2, 768, 1536], P('section', 'dp'), may hold values from -2.5 to 2.5
- in_weight: bfloat16 [2, 768, 4096], P('section', 'dp'), may hold values from -0.21875 to 0.21875
- down_weight: bfloat16 [2, 2048, 768], P('section', 'dp'), may hold values from -0.125 to 0.125
Outputs:
- block_out: bfloat16 [2, 32, 256, 768], P('section', 'dp')
- input_grad: float32 [2, 32, 256, 768], P('section', 'dp')
- gains_grad: float32 [2, 3, 768], P('section', None, 'dp')
- qkv_grad: float32 [2, 768, 2304], P('section', 'dp')
- out_grad: float32 [2, 768, 768], P('section', 'dp')
- cross_grad: float32 [2, 768, 1536], P('section', 'dp')
- in_grad: float32 [2, 768, 4096], P('section', 'dp')
- down_grad: float32 [2, 2048, 768], P('section', 'dp')
Inputs may be any that keep to these rules, and one draw needn't show every extreme that they name: `lengths`: in every draw some table has exactly 256 tokens.
All inputs are finite; a program needn't handle non-finite values.
Results may differ from a plain program's by a relative error of at most 0.015.
Values may be sent and summed in bfloat16 or wider, within the bound.
A program may use at most 384 MiB of HBM per device.

v0:
```python
from functools import partial

import jax
import jax.numpy as jnp
from jax import lax
from jax.sharding import PartitionSpec as P

HEADS = 12
HEAD_DIM = 64


EPS = 1e-06
NEG = -1000000000.0


def shifted(block, axis, distance):
    devices = range(lax.axis_size(axis))
    route = [(i - distance, i) for i in devices if i - distance in devices]
    return lax.ppermute(block, axis, route)


def product(a, b):
    return jnp.dot(a, b, preferred_element_type=jnp.float32)


def split_heads(v):
    return v.reshape(v.shape[0], HEADS, -1)


def norm_forward(h, norm_gain):
    inv_root = lax.rsqrt(jnp.mean(h * h, axis=-1, keepdims=True) + EPS)
    return (h * inv_root * norm_gain.astype(jnp.float32), inv_root)


def norm_back(d_normed, h, inv_root, norm_gain):
    scaled = h * inv_root
    d_gain = jnp.sum(d_normed * scaled, axis=0)
    inner = d_normed * norm_gain.astype(jnp.float32)
    d_input = inv_root * (inner - scaled * jnp.mean(inner * scaled, axis=-1, keepdims=True))
    return (d_input, d_gain)


def score_block(q, k, key_mask):
    scores = jnp.einsum(
        "qhd,khd->hqk", split_heads(q), split_heads(k), preferred_element_type=jnp.float32
    ) * HEAD_DIM ** (-0.5)
    if key_mask is not None:
        scores = jnp.where(key_mask[None], scores, NEG)
    return scores


def attend_forward(q, k, v, key_mask):
    scores = score_block(q, k, key_mask)
    highest = jnp.max(scores, axis=-1, keepdims=True)
    expo = jnp.exp(scores - highest)
    total = jnp.sum(expo, axis=-1, keepdims=True)
    weights = (expo / total).astype(jnp.bfloat16)
    output = jnp.einsum("hqk,khd->qhd", weights, split_heads(v), preferred_element_type=jnp.float32)
    return (output.reshape(q.shape[0], -1), highest + jnp.log(total))


def attend_back(q, k, v, key_mask, log_total, d_out):
    scores = score_block(q, k, key_mask)
    probs = jnp.exp(scores - log_total)
    heads_dout = split_heads(d_out)
    d_value = jnp.einsum(
        "hqk,qhd->khd", probs.astype(jnp.bfloat16), heads_dout, preferred_element_type=jnp.float32
    )
    d_probs = jnp.einsum(
        "qhd,khd->hqk", heads_dout, split_heads(v), preferred_element_type=jnp.float32
    )
    centre = jnp.sum(probs * d_probs, axis=-1, keepdims=True)
    d_scores = (probs * (d_probs - centre)).astype(jnp.bfloat16)
    d_query = jnp.einsum(
        "hqk,khd->qhd", d_scores, split_heads(k), preferred_element_type=jnp.float32
    ) * HEAD_DIM ** (-0.5)
    d_key = jnp.einsum(
        "hqk,qhd->khd", d_scores, split_heads(q), preferred_element_type=jnp.float32
    ) * HEAD_DIM ** (-0.5)
    rows_query = q.shape[0]
    rows_key = k.shape[0]
    return (
        d_query.reshape(rows_query, -1),
        d_key.reshape(rows_key, -1),
        d_value.reshape(rows_key, -1),
    )


def attention_forward(h, norm_gain, w_qkv, w_out, key_mask):
    normed, inv_root = norm_forward(h, norm_gain)
    normed_low = normed.astype(jnp.bfloat16)
    joined = product(normed_low, w_qkv).astype(jnp.bfloat16)
    q, k, v = jnp.split(joined, 3, axis=1)
    output, log_total = attend_forward(q, k, v, key_mask)
    output_low = output.astype(jnp.bfloat16)
    return (normed_low, inv_root, joined, output_low, log_total, product(output_low, w_out))


def attention_back(d_h, h, saved, norm_gain, w_qkv, w_out, key_mask):
    normed_low, inv_root, joined, output_low, log_total, unused = saved
    d_low = d_h.astype(jnp.bfloat16)
    d_wout = product(output_low.T, d_low)
    d_output = product(d_low, w_out.T).astype(jnp.bfloat16)
    q, k, v = jnp.split(joined, 3, axis=1)
    d_query, d_key, d_value = attend_back(q, k, v, key_mask, log_total, d_output)
    d_joined = jnp.concatenate([d_query, d_key, d_value], axis=1).astype(jnp.bfloat16)
    d_wqkv = product(normed_low.T, d_joined)
    d_normed = product(d_joined, w_qkv.T)
    d_input, d_gain = norm_back(d_normed, h, inv_root, norm_gain)
    return (d_input, d_gain, d_wqkv, d_wout)


def mlp_forward(h, norm_gain, w_in, w_down):
    normed, inv_root = norm_forward(h, norm_gain)
    normed_low = normed.astype(jnp.bfloat16)
    joined = product(normed_low, w_in)
    gate, upper = jnp.split(joined, 2, axis=1)
    hidden_low = (jax.nn.gelu(gate, approximate=True) * upper).astype(jnp.bfloat16)
    return (normed_low, inv_root, joined, hidden_low, product(hidden_low, w_down))


def mlp_back(d_h, h, saved, norm_gain, w_in, w_down):
    normed_low, inv_root, joined, hidden_low, unused = saved
    d_low = d_h.astype(jnp.bfloat16)
    d_wdown = product(hidden_low.T, d_low)
    d_hidden = product(d_low, w_down.T)
    gate, upper = jnp.split(joined, 2, axis=1)
    active, active_back = jax.vjp(partial(jax.nn.gelu, approximate=True), gate)
    d_gate = active_back(d_hidden * upper)[0]
    d_upper = d_hidden * active
    d_joined = jnp.concatenate([d_gate, d_upper], axis=1).astype(jnp.bfloat16)
    d_win = product(normed_low.T, d_joined)
    d_normed = product(d_joined, w_in.T)
    d_input, d_gain = norm_back(d_normed, h, inv_root, norm_gain)
    return (d_input, d_gain, d_win, d_wdown)


def encoder_forward(weights, source):
    gains, w_qkv, w_out, w_cross, w_in, w_down = weights
    inputs = source.astype(jnp.float32)
    attn_saved = attention_forward(inputs, gains[0], w_qkv, w_out, None)
    middle = inputs + attn_saved[-1]
    mlp_saved = mlp_forward(middle, gains[1], w_in, w_down)
    final = middle + mlp_saved[-1]
    normed, inv_root = norm_forward(final, gains[2])
    memory = normed.astype(jnp.bfloat16)
    key_value = product(memory, w_cross).astype(jnp.bfloat16)
    return (inputs, attn_saved, middle, mlp_saved, final, inv_root, memory, key_value)


def encoder_front(weights, source):
    saved = encoder_forward(weights, source)
    return (saved[7], saved[6])


def encoder_back_saved(weights, saved, d_keyvalue):
    gains, w_qkv, w_out, w_cross, w_in, w_down = weights
    inputs, attn_saved, middle, mlp_saved, final, inv_root, memory, key_value = saved
    d_wcross = product(memory.T, d_keyvalue)
    d_memory = product(d_keyvalue, w_cross.T)
    d_final, gain_last = norm_back(d_memory, final, inv_root, gains[2])
    d_part, gain_mlp, d_win, d_wdown = mlp_back(d_final, middle, mlp_saved, gains[1], w_in, w_down)
    d_middle = d_final + d_part
    d_first, gain_attn, d_wqkv, d_wout = attention_back(
        d_middle, inputs, attn_saved, gains[0], w_qkv, w_out, None
    )
    grads = (jnp.stack([gain_attn, gain_mlp, gain_last]), d_wqkv, d_wout, d_wcross, d_win, d_wdown)
    return (d_middle + d_first, grads)


def encoder_back(weights, source, d_keyvalue):
    return encoder_back_saved(weights, encoder_forward(weights, source), d_keyvalue)


def decoder_pass(weights, source, key_value, weight_cot, length, factor):
    gains, w_qkv, w_out, w_cross, w_in, w_down = weights
    width = source.shape[1]
    inputs = source.astype(jnp.float32)
    position = jnp.arange(inputs.shape[0], dtype=jnp.int32)
    is_valid = position < length
    key_mask = (position[None, :] <= position[:, None]) & is_valid[None, :]
    attn_saved = attention_forward(inputs, gains[0], w_qkv, w_out, key_mask)
    middle = inputs + attn_saved[-1]
    normed, inv_root = norm_forward(middle, gains[1])
    normed_low = normed.astype(jnp.bfloat16)
    w_query = w_cross[:, :width]
    w_back = w_cross[:, width:]
    queries = product(normed_low, w_query).astype(jnp.bfloat16)
    mem_keys = key_value[:, :width]
    mem_values = key_value[:, width:]
    cross_out, cross_total = attend_forward(queries, mem_keys, mem_values, None)
    cross_low = cross_out.astype(jnp.bfloat16)
    after = middle + product(cross_low, w_back)
    mlp_saved = mlp_forward(after, gains[2], w_in, w_down)
    final = after + mlp_saved[-1]
    d_final = jnp.where(is_valid[:, None], weight_cot.astype(jnp.float32) * factor, 0.0)
    d_part, gain_mlp, d_win, d_wdown = mlp_back(d_final, after, mlp_saved, gains[2], w_in, w_down)
    d_after = d_final + d_part
    d_low = d_after.astype(jnp.bfloat16)
    d_wback = product(cross_low.T, d_low)
    d_cross = product(d_low, w_back.T).astype(jnp.bfloat16)
    d_query, d_key, d_value = attend_back(queries, mem_keys, mem_values, None, cross_total, d_cross)
    d_query_low = d_query.astype(jnp.bfloat16)
    d_wquery = product(normed_low.T, d_query_low)
    d_normed = product(d_query_low, w_query.T)
    d_norm_in, gain_cross = norm_back(d_normed, middle, inv_root, gains[1])
    d_middle = d_after + d_norm_in
    d_keyvalue = jnp.concatenate([d_key, d_value], axis=1).astype(jnp.bfloat16)
    d_first, gain_attn, d_wqkv, d_wout = attention_back(
        d_middle, inputs, attn_saved, gains[0], w_qkv, w_out, key_mask
    )
    grads = (
        jnp.stack([gain_attn, gain_cross, gain_mlp]),
        d_wqkv,
        d_wout,
        jnp.concatenate([d_wquery, d_wback], axis=1),
        d_win,
        d_wdown,
    )
    return (final.astype(jnp.bfloat16), d_middle + d_first, d_keyvalue, grads)


def on_section(flag, work, operands):

    def run_work(values):
        return work(*values)

    def skip_work(values):
        return jax.tree.map(jnp.zeros_like, work(*values))

    return lax.cond(flag, run_work, skip_work, operands)


def body(
    block_in,
    cotangent,
    lengths,
    sources,
    loss_weight,
    gains,
    qkv_weight,
    out_weight,
    cross_weight,
    in_weight,
    down_weight,
):
    is_encoder = lax.axis_index("section") == 0
    is_decoder = jnp.logical_not(is_encoder)
    wide = lax.axis_size("dp")
    gathered = (
        lax.all_gather(gains, "dp", axis=2, tiled=True),
        lax.all_gather(qkv_weight, "dp", axis=1, tiled=True),
        lax.all_gather(out_weight, "dp", axis=1, tiled=True),
        lax.all_gather(cross_weight, "dp", axis=1, tiled=True),
        lax.all_gather(in_weight, "dp", axis=1, tiled=True),
        lax.all_gather(down_weight, "dp", axis=1, tiled=True),
    )
    weights = tuple((w[0] for w in gathered))
    onehot = (sources[:, None] == jnp.arange(3, dtype=jnp.int32)[None, :]).astype(jnp.float32)
    counts = lax.psum(jnp.sum(onehot * lengths[:, None].astype(jnp.float32), axis=0), "dp")
    own_count = jnp.sum(onehot * counts[None, :], axis=1)
    own_weight = jnp.sum(onehot * loss_weight[None, :].astype(jnp.float32), axis=1)
    scale = own_weight * (lengths.shape[0] * wide * block_in.shape[2] / 3.0) / own_count

    def step(carry, item):
        source, weight_cot, length, factor = item
        key_value, memory = on_section(is_encoder, encoder_front, (weights, source))
        received = shifted(key_value, "section", 1)
        decoded, table_grad, d_keyvalue, dec_grads = on_section(
            is_decoder, decoder_pass, (weights, source, received, weight_cot, length, factor)
        )
        returned = shifted(d_keyvalue, "section", -1)
        plot_grad, enc_grads = on_section(is_encoder, encoder_back, (weights, source, returned))
        grads = tuple((a + b for a, b in zip(dec_grads, enc_grads)))
        carry = tuple((a + b for a, b in zip(carry, grads)))
        return (carry, (memory + decoded, plot_grad + table_grad))

    start = tuple((jnp.zeros(w.shape, jnp.float32) for w in weights))
    carry, (outputs, input_grads) = lax.scan(step, start, (block_in[0], cotangent, lengths, scale))
    gain_total, qkv_total, out_total, cross_sum, in_total, down_total = carry
    reduced = (
        lax.psum_scatter(gain_total[None], "dp", scatter_dimension=2, tiled=True),
        lax.psum_scatter(qkv_total[None], "dp", scatter_dimension=1, tiled=True),
        lax.psum_scatter(out_total[None], "dp", scatter_dimension=1, tiled=True),
        lax.psum_scatter(cross_sum[None], "dp", scatter_dimension=1, tiled=True),
        lax.psum_scatter(in_total[None], "dp", scatter_dimension=1, tiled=True),
        lax.psum_scatter(down_total[None], "dp", scatter_dimension=1, tiled=True),
    )
    return (
        outputs[None],
        input_grads[None],
        reduced[0],
        reduced[1],
        reduced[2],
        reduced[3],
        reduced[4],
        reduced[5],
    )


def solution(mesh):
    in_specs = (
        P("section", "dp", None, None),
        P("dp", None, None),
        P("dp"),
        P("dp"),
        P(),
        P("section", None, "dp"),
        P("section", "dp", None),
        P("section", "dp", None),
        P("section", "dp", None),
        P("section", "dp", None),
        P("section", "dp", None),
    )
    out_specs = (
        P("section", "dp", None, None),
        P("section", "dp", None, None),
        P("section", None, "dp"),
        P("section", "dp", None),
        P("section", "dp", None),
        P("section", "dp", None),
        P("section", "dp", None),
        P("section", "dp", None),
    )
    return jax.shard_map(body, mesh=mesh, in_specs=in_specs, out_specs=out_specs, check_vma=False)
```

profile of v0, /device:TPU:0, one launch (start us, length us, event | category | flops | bytes accessed | tf_op | source)
XLA Modules:
  0.0 1324.0 jit_solution(9207465354891030654)
XLA Ops:
  12.0 35.1 %psum.7 = f32[3]{0:T(128)S(1)} all-reduce(f32[3]{0:T(128)S(1)} %select_reduce_fusion.1), channel_id=1, replica_groups=mesh['section'=2,'dp'=16] {'dp'}, use_global_device_ids=true, to_apply=%region_2.0 | all-reduce | flops 3 | bytes 24 | tf_op jit(solution)/shard_map/psum | solution.py:260
  48.6 18.4 %all_gather.18 = bf16[1,3,768]{1,0,2:T(2,128)(2,1)S(1)} all-gather(bf16[1,3,48]{1,0,2:T(2,128)(2,1)S(1)} %copy.178), channel_id=1, replica_groups=mesh['section'=2,'dp'=16] {'dp'}, dimensions={2}, use_global_device_ids=true | all-gather | bytes 4896 | tf_op jit(solution)/shard_map/all_gather | solution.py:251
  68.2 26.8 %all-gather.14.cloned.1.call-done = bf16[1,768,1536]{2,1,0:T(8,128)(2,1)} async-done(((bf16[1,48,1536]{2,1,0:T(8,128)(2,1)}), bf16[1,768,1536]{2,1,0:T(8,128)(2,1)}) %all-gather.14.cloned.1.call-update) | async-done | bytes 2359312 | tf_op jit(solution)/shard_map/all_gather | solution.py:254
  95.0 46.3 %all-gather.12.cloned.1.call-done = bf16[1,2048,768]{2,1,0:T(8,128)(2,1)} async-done(((bf16[1,128,768]{2,1,0:T(8,128)(2,1)}), bf16[1,2048,768]{2,1,0:T(8,128)(2,1)}) %all-gather.12.cloned.1.call-update) | async-done | bytes 3145744 | tf_op jit(solution)/shard_map/all_gather | solution.py:256
  141.3 48.2 %all-gather.6.cloned.1.call-done = bf16[1,768,2304]{2,1,0:T(8,128)(2,1)} async-done(((bf16[1,48,2304]{2,1,0:T(8,128)(2,1)}), bf16[1,768,2304]{2,1,0:T(8,128)(2,1)}) %all-gather.6.cloned.1.call-update) | async-done | bytes 3538960 | tf_op jit(solution)/shard_map/all_gather | solution.py:252
  189.5 63.0 %all-gather.10.cloned.1.call-done = bf16[1,768,4096]{2,1,0:T(8,128)(2,1)} async-done(((bf16[1,48,4096]{2,1,0:T(8,128)(2,1)}), bf16[1,768,4096]{2,1,0:T(8,128)(2,1)}) %all-gather.10.cloned.1.call-update) | async-done | bytes 6291472 | tf_op jit(solution)/shard_map/all_gather | solution.py:255
  252.5 539.7 %while.25 = (s32[]{:T(128)}, f32[3,768]{1,0:T(4,128)}, f32[768,2304]{1,0:T(8,128)}, f32[768,768]{1,0:T(8,128)}, f32[768,1536]{1,0:T(8,128)}, /*index=5*/f32[768,...) while((s32[]{:T(128)}, f32[3,768]{1,0:T(4,128)}, ...), condition=%wide.region_43.44_spmd.clone, body=%wide.region_4.43_spmd.clone.sunk | while | flops 31191597056 | bytes 995728576 | solution.py:279
  253.5 18.3 %conditional.9 = (bf16[256,1536]{1,0:T(8,128)(2,1)S(1)}, bf16[256,768]{1,0:T(8,128)(2,1)}) conditional(s32[]{:T(128)} %convert_element_type.445, () %tuple.112, (bf16[256,768]{1,0:T(8,128)(2,1)S(1)}, bf16[3,768]{1,0:T(4,128)(2,1)S(1)}, bf16[768,2304]{1,0:T(8,128)(2,1)}, bf16[768,768]{1,0:T(8,128)(2,1)}, bf16[768,4096]{1,0:T(8,128)(2,1)}, ...), branch_computations={%region_5.5_spmd, %region_6.11_spmd} | conditional | flops 4443474944 | bytes 91417240 | solution.py:231
  253.7 3.1 convolution_convert_fusion
  258.2 4.0 fusion.170
  262.2 2.4 fusion.15
  273.4 17.4 %collective-permute-done = bf16[256,1536]{0,1:T(8,128)(2,1)S(1)} collective-permute-done((bf16[256,1536]{0,1:T(8,128)(2,1)S(1)}, bf16[256,1536]{0,1:T(8,128)(2,1)S(1)}, u32[]{:S(2)}, u32[]{:S(2)}) %collective-permute-start) | collective-permute-done | bytes 786464 | tf_op jit(solution)/shard_map/while/body/eval_jaxpr/ppermute | solution.py:19
  290.9 22.8 %conditional.10 = (bf16[256,768]{1,0:T(8,128)(2,1)}, f32[256,768]{1,0:T(8,128)}, bf16[256,1536]{0,1:T(8,128)(2,1)}, f32[3,768]{1,0:T(4,128)}, f32[768,2304]{1,0:...) conditional(s32[]{:T(128)} %convert_element_type.444, ...), branch_computations={%region_12.12_spmd, %region_13.28_spmd} | conditional | flops 13973643264 | bytes 421253344 | solution.py:231
  295.6 2.7 broadcast.339.clone
  298.4 3.0 broadcast.341
  301.4 3.3 broadcast.337
  304.7 6.1 broadcast.340
  316.4 2.0 bitcast_dynamic-update-slice_fusion.4
  318.4 92.1 %collective-permute-done.1 = bf16[256,1536]{1,0:T(8,128)(2,1)S(1)} collective-permute-done((bf16[256,1536]{1,0:T(8,128)(2,1)S(1)}, bf16[256,1536]{1,0:T(8,128)(2,1)S(1)}, u32[]{:S(2)}, u32[]{:S(2)}) %collective-permute-start.1) | collective-permute-done | bytes 786464 | tf_op jit(solution)/shard_map/while/body/eval_jaxpr/ppermute | solution.py:19
  410.4 59.6 %conditional.11 = (f32[256,768]{1,0:T(8,128)}, f32[3,768]{1,0:T(4,128)S(1)}, f32[768,2304]{1,0:T(8,128)}, f32[768,768]{1,0:T(8,128)}, f32[768,1536]{1,0:T(8,128)...) conditional(s32[]{:T(128)} %convert_element_type.445, () %tuple.115, (bf16[256,768]{1,0:T(8,128)(2,1)S(1)}, ...), branch_computations={%region_29.29_spmd, %region_30.42_spmd} | conditional | flops 12748716032 | bytes 285121280 | solution.py:231
  412.1 3.1 convolution_convert_fusion.6
  431.6 2.8 fusion.122
  434.4 2.0 multiply_reduce_fusion.15
  452.2 3.2 fusion.150
  455.4 3.8 fusion.156
  459.2 4.1 fusion.148
  463.4 6.5 fusion.129
  470.0 8.5 select_add_fusion.17
  478.5 15.9 %select_add_fusion.16 = f32[768,4096]{1,0:T(8,128)} fusion(f32[768,4096]{1,0:T(8,128)} %get-tuple-element.736, f32[768,4096]{1,0:T(8,128)} %get-tuple-element.664, f32[768,4096]{1,0:T(8,128)} %get-tuple-element.665, pred[]{:T(512)S(6)} %compare.3), kind=kLoop, calls=%fused_computation.270.clone.1 | loop fusion | flops 9437184 | bytes 50331648 | tf_op jit(solution)/shard_map/while/body/eval_jaxpr/add | solution.py:275
  494.5 6.9 select_add_fusion.15
  501.4 5.6 select_add_fusion.14
  507.8 9.2 select_add_fusion.13
  517.0 2.3 bitcast_dynamic-update-slice_fusion.5
  520.7 18.3 %conditional.9 = (bf16[256,1536]{1,0:T(8,128)(2,1)S(1)}, bf16[256,768]{1,0:T(8,128)(2,1)}) conditional(s32[]{:T(128)} %convert_element_type.445, () %tuple.112, (bf16[256,768]{1,0:T(8,128)(2,1)S(1)}, bf16[3,768]{1,0:T(4,128)(2,1)S(1)}, bf16[768,2304]{1,0:T(8,128)(2,1)}, bf16[768,768]{1,0:T(8,128)(2,1)}, bf16[768,4096]{1,0:T(8,128)(2,1)}, ...), branch_computations={%region_5.5_spmd, %region_6.11_spmd} | conditional | flops 4443474944 | bytes 91417240 | solution.py:231
  520.9 3.1 convolution_convert_fusion
  525.4 4.0 fusion.170
  529.4 2.4 fusion.15
  540.6 16.4 %collective-permute-done = bf16[256,1536]{0,1:T(8,128)(2,1)S(1)} collective-permute-done((bf16[256,1536]{0,1:T(8,128)(2,1)S(1)}, bf16[256,1536]{0,1:T(8,128)(2,1)S(1)}, u32[]{:S(2)}, u32[]{:S(2)}) %collective-permute-start) | collective-permute-done | bytes 786464 | tf_op jit(solution)/shard_map/while/body/eval_jaxpr/ppermute | solution.py:19
  556.9 23.1 %conditional.10 = (bf16[256,768]{1,0:T(8,128)(2,1)}, f32[256,768]{1,0:T(8,128)}, bf16[256,1536]{0,1:T(8,128)(2,1)}, f32[3,768]{1,0:T(4,128)}, f32[768,2304]{1,0:...) conditional(s32[]{:T(128)} %convert_element_type.444, ...), branch_computations={%region_12.12_spmd, %region_13.28_spmd} | conditional | flops 13973643264 | bytes 421253344 | solution.py:231
  561.7 2.7 broadcast.339.clone
  564.4 3.0 broadcast.341
  567.5 3.3 broadcast.337
  570.8 6.1 broadcast.340
  584.7 90.3 %collective-permute-done.1 = bf16[256,1536]{1,0:T(8,128)(2,1)S(1)} collective-permute-done((bf16[256,1536]{1,0:T(8,128)(2,1)S(1)}, bf16[256,1536]{1,0:T(8,128)(2,1)S(1)}, u32[]{:S(2)}, u32[]{:S(2)}) %collective-permute-start.1) | collective-permute-done | bytes 786464 | tf_op jit(solution)/shard_map/while/body/eval_jaxpr/ppermute | solution.py:19
  675.0 59.5 %conditional.11 = (f32[256,768]{1,0:T(8,128)}, f32[3,768]{1,0:T(4,128)S(1)}, f32[768,2304]{1,0:T(8,128)}, f32[768,768]{1,0:T(8,128)}, f32[768,1536]{1,0:T(8,128)...) conditional(s32[]{:T(128)} %convert_element_type.445, () %tuple.115, (bf16[256,768]{1,0:T(8,128)(2,1)S(1)}, ...), branch_computations={%region_29.29_spmd, %region_30.42_spmd} | conditional | flops 12748716032 | bytes 285121280 | solution.py:231
  676.6 3.1 convolution_convert_fusion.6
  696.0 2.6 fusion.122
  698.6 2.0 multiply_reduce_fusion.15
  716.4 3.2 fusion.150
  719.6 3.8 fusion.156
  723.4 4.1 fusion.148
  727.6 6.5 fusion.129
  734.5 10.2 select_add_fusion.17
  744.7 18.6 %select_add_fusion.16 = f32[768,4096]{1,0:T(8,128)} fusion(f32[768,4096]{1,0:T(8,128)} %get-tuple-element.736, f32[768,4096]{1,0:T(8,128)} %get-tuple-element.664, f32[768,4096]{1,0:T(8,128)} %get-tuple-element.665, pred[]{:T(512)S(6)} %compare.3), kind=kLoop, calls=%fused_computation.270.clone.1 | loop fusion | flops 9437184 | bytes 50331648 | tf_op jit(solution)/shard_map/while/body/eval_jaxpr/add | solution.py:275
  763.4 6.9 select_add_fusion.15
  770.3 5.6 select_add_fusion.14
  776.8 11.2 select_add_fusion.13
  788.0 2.3 bitcast_dynamic-update-slice_fusion.5
  798.9 50.0 %reduce-scatter.19.cloned.1.call-done = f32[48,3]{1,0:T(8,128)} async-done(((f32[768,3]{1,0:T(8,128)}), f32[48,3]{1,0:T(8,128)}) %reduce-scatter.19.cloned.1.call-update) | async-done | bytes 592
  850.4 65.3 %reduce-scatter.11.cloned.1.call-done = f32[1,48,768]{2,1,0:T(8,128)} async-done(((f32[1,768,768]{2,1,0:T(8,128)}), f32[1,48,768]{2,1,0:T(8,128)}) %reduce-scatter.11.cloned.1.call-update) | async-done | bytes 147472 | tf_op jit(solution)/shard_map/reduce_scatter | solution.py:284
  915.7 79.1 %reduce-scatter.13.cloned.1.call-done = f32[1,48,1536]{2,1,0:T(8,128)} async-done(((f32[1,768,1536]{2,1,0:T(8,128)}), f32[1,48,1536]{2,1,0:T(8,128)}) %reduce-scatter.13.cloned.1.call-update) | async-done | bytes 294928 | tf_op jit(solution)/shard_map/reduce_scatter | solution.py:285
  994.8 89.3 %reduce-scatter.17.cloned.1.call-done = f32[1,128,768]{2,1,0:T(8,128)} async-done(((f32[1,2048,768]{2,1,0:T(8,128)}), f32[1,128,768]{2,1,0:T(8,128)}) %reduce-scatter.17.cloned.1.call-update) | async-done | bytes 393232 | tf_op jit(solution)/shard_map/reduce_scatter | solution.py:287
  1084.0 93.7 %reduce-scatter.9.cloned.1.call-done = f32[1,48,2304]{2,1,0:T(8,128)} async-done(((f32[1,768,2304]{2,1,0:T(8,128)}), f32[1,48,2304]{2,1,0:T(8,128)}) %reduce-scatter.9.cloned.1.call-update) | async-done | bytes 442384 | tf_op jit(solution)/shard_map/reduce_scatter | solution.py:283
  1177.7 139.5 %reduce-scatter.15.cloned.1.call-done = f32[1,48,4096]{2,1,0:T(8,128)} async-done(((f32[1,768,4096]{2,1,0:T(8,128)}), f32[1,48,4096]{2,1,0:T(8,128)}) %reduce-scatter.15.cloned.1.call-update) | async-done | bytes 786448 | tf_op jit(solution)/shard_map/reduce_scatter | solution.py:286
  (398 shorter events, 123.0 us)
Async XLA Ops:
  7.2 61.0 %all-gather.8.cloned.1.call-start = ((), (), s32[]{:S(2)}) async-start(), calls=%async_computation.7 | async-start | bytes 1253376 | tf_op jit(solution)/shard_map/all_gather | solution.py:253
  7.9 87.1 %all-gather.14.cloned.1.call-start = ((), (), s32[]{:S(2)}) async-start(), calls=%async_computation.10 | async-start | bytes 2506752 | tf_op jit(solution)/shard_map/all_gather | solution.py:254
  8.6 132.6 %all-gather.12.cloned.1.call-start = ((), (), s32[]{:S(2)}) async-start(), calls=%async_computation.9 | async-start | bytes 3342336 | tf_op jit(solution)/shard_map/all_gather | solution.py:256
  9.4 180.1 %all-gather.6.cloned.1.call-start = ((), (), s32[]{:S(2)}) async-start(), calls=%async_computation.6 | async-start | bytes 3760128 | tf_op jit(solution)/shard_map/all_gather | solution.py:252
  10.0 242.5 %all-gather.10.cloned.1.call-start = ((), (), s32[]{:S(2)}) async-start(), calls=%async_computation.8 | async-start | bytes 6684672 | tf_op jit(solution)/shard_map/all_gather | solution.py:255
  10.5 838.3 %reduce-scatter.19.cloned.1.call-start = ((), (), s32[]{:S(2)}) async-start(), calls=%async_computation.16 | async-start | bytes 417792
  252.5 38.4 %copy-start.108 = (f32[2]{0:T(128)}, f32[2]{0:T(128)S(1)}, u32[]{:S(2)}) copy-start(f32[2]{0:T(128)S(1)} %get-tuple-element.774) | copy-start | bytes 28 | tf_op jit(solution)/shard_map/while
  252.5 158.0 %copy-start.76 = (bf16[3,768]{1,0:T(4,128)(2,1)}, bf16[3,768]{1,0:T(4,128)(2,1)S(1)}, u32[]{:S(2)}) copy-start(bf16[3,768]{1,0:T(4,128)(2,1)S(1)} %get-tuple-element.766) | copy-start | bytes 13828 | tf_op jit(solution)/shard_map/while
  253.5 37.4 %copy-start.107 = (s32[2]{0:T(128)S(1)}, s32[2]{0:T(128)}, u32[]{:S(2)}) copy-start(s32[2]{0:T(128)} %get-tuple-element.772) | copy-start | bytes 28 | tf_op jit(solution)/shard_map/while
  258.2 7.1 slice-start
  262.2 3.5 slice-start.1
  272.1 18.8 %collective-permute-start = (bf16[256,1536]{0,1:T(8,128)(2,1)S(1)}, bf16[256,1536]{0,1:T(8,128)(2,1)S(1)}, u32[]{:S(2)}, u32[]{:S(2)}) collective-permute-start(bf16[256,1536]{0,1:T(8,128)(2,1)S(1)} %copy.199), channel_id=1, source_target_pairs={{0,16},{1,17},{2,18},{3,19},{4,20},{5,21},{6,22},{7,23},{8,24},{9,... | collective-permute-start | bytes 2359304 | tf_op jit(solution)/shard_map/while/body/eval_jaxpr/ppermute | solution.py:19
  315.1 95.3 %collective-permute-start.1 = (bf16[256,1536]{1,0:T(8,128)(2,1)S(1)}, bf16[256,1536]{1,0:T(8,128)(2,1)S(1)}, u32[]{:S(2)}, u32[]{:S(2)}) collective-permute-start(bf16[256,1536]{1,0:T(8,128)(2,1)S(1)} %copy.200), channel_id=1, source_target_pairs={{16,0},{17,1},{18,2},{19,3},{20,4},{21,5},{22,6},{23,7},{24,8},{25... | collective-permute-start | bytes 2359304 | tf_op jit(solution)/shard_map/while/body/eval_jaxpr/ppermute | solution.py:19
  411.3 4.1 copy-start.89
  423.1 14.0 %copy-start.8 = (f32[256,768]{1,0:T(8,128)}, f32[256,768]{1,0:T(8,128)S(1)}, u32[]{:S(2)}) copy-start(f32[256,768]{1,0:T(8,128)S(1)} %get-tuple-element.501) | copy-start | bytes 2359300 | tf_op jit(solution)/shard_map/while/body/eval_jaxpr/cond
  427.3 3.4 copy-start.24
  431.6 5.5 copy-start.21
  441.4 3.8 copy-start.35
  441.4 3.8 copy-start.50
  441.4 3.8 copy-start.74
  459.2 4.1 copy-start.9
  459.2 4.1 copy-start.65
  459.2 4.1 copy-start.67
  463.4 6.5 copy-start.81
  478.5 15.9 %slice-start.6 = ((s8[4718592]{0:T(1024)(128)(4,1)}), s8[4194304]{0:T(1024)(128)(4,1)S(1)}, s32[]{:S(2)}) async-start(s8[4718592]{0:T(1024)(128)(4,1)} %bitcast.181), calls=%async_computation.23 | async-start | bytes 8388608 | tf_op jit(solution)/shard_map/while
  478.5 15.9 %slice-start.7 = ((s8[4718592]{0:T(1024)(128)(4,1)}), s8[524288]{0:T(1024)(128)(4,1)S(1)}, s32[]{:S(2)}) async-start(s8[4718592]{0:T(1024)(128)(4,1)} %bitcast.181), calls=%async_computation.24 | async-start | bytes 1048576 | tf_op jit(solution)/shard_map/while
  494.4 7.0 copy-start.37
  501.4 5.6 copy-start.23
  501.4 5.6 copy-start.85
  507.0 10.0 copy-start.38
  507.8 9.2 copy-start.86
  507.8 11.6 copy-start.77
  507.8 11.6 copy-start.109
  519.6 37.3 %copy-start.108 = (f32[2]{0:T(128)}, f32[2]{0:T(128)S(1)}, u32[]{:S(2)}) copy-start(f32[2]{0:T(128)S(1)} %get-tuple-element.774) | copy-start | bytes 28 | tf_op jit(solution)/shard_map/while
  519.6 155.4 %copy-start.76 = (bf16[3,768]{1,0:T(4,128)(2,1)}, bf16[3,768]{1,0:T(4,128)(2,1)S(1)}, u32[]{:S(2)}) copy-start(bf16[3,768]{1,0:T(4,128)(2,1)S(1)} %get-tuple-element.766) | copy-start | bytes 13828 | tf_op jit(solution)/shard_map/while
  520.6 36.3 %copy-start.107 = (s32[2]{0:T(128)S(1)}, s32[2]{0:T(128)}, u32[]{:S(2)}) copy-start(s32[2]{0:T(128)} %get-tuple-element.772) | copy-start | bytes 28 | tf_op jit(solution)/shard_map/while
  525.4 7.1 slice-start
  529.4 3.5 slice-start.1
  539.2 17.7 %collective-permute-start = (bf16[256,1536]{0,1:T(8,128)(2,1)S(1)}, bf16[256,1536]{0,1:T(8,128)(2,1)S(1)}, u32[]{:S(2)}, u32[]{:S(2)}) collective-permute-start(bf16[256,1536]{0,1:T(8,128)(2,1)S(1)} %copy.199), channel_id=1, source_target_pairs={{0,16},{1,17},{2,18},{3,19},{4,20},{5,21},{6,22},{7,23},{8,24},{9,... | collective-permute-start | bytes 2359304 | tf_op jit(solution)/shard_map/while/body/eval_jaxpr/ppermute | solution.py:19
  581.4 93.5 %collective-permute-start.1 = (bf16[256,1536]{1,0:T(8,128)(2,1)S(1)}, bf16[256,1536]{1,0:T(8,128)(2,1)S(1)}, u32[]{:S(2)}, u32[]{:S(2)}) collective-permute-start(bf16[256,1536]{1,0:T(8,128)(2,1)S(1)} %copy.200), channel_id=1, source_target_pairs={{16,0},{17,1},{18,2},{19,3},{20,4},{21,5},{22,6},{23,7},{24,8},{25... | collective-permute-start | bytes 2359304 | tf_op jit(solution)/shard_map/while/body/eval_jaxpr/ppermute | solution.py:19
  675.7 4.1 copy-start.89
  687.5 13.7 %copy-start.8 = (f32[256,768]{1,0:T(8,128)}, f32[256,768]{1,0:T(8,128)S(1)}, u32[]{:S(2)}) copy-start(f32[256,768]{1,0:T(8,128)S(1)} %get-tuple-element.501) | copy-start | bytes 2359300 | tf_op jit(solution)/shard_map/while/body/eval_jaxpr/cond
  696.0 5.2 copy-start.21
  705.6 3.8 copy-start.35
  705.6 3.8 copy-start.50
  705.6 3.8 copy-start.74
  723.4 4.1 copy-start.9
  723.4 4.1 copy-start.65
  723.4 4.1 copy-start.67
  727.5 6.5 copy-start.81
  744.7 18.7 %slice-start.6 = ((s8[4718592]{0:T(1024)(128)(4,1)}), s8[4194304]{0:T(1024)(128)(4,1)S(1)}, s32[]{:S(2)}) async-start(s8[4718592]{0:T(1024)(128)(4,1)} %bitcast.181), calls=%async_computation.23 | async-start | bytes 8388608 | tf_op jit(solution)/shard_map/while
  744.7 18.7 %slice-start.7 = ((s8[4718592]{0:T(1024)(128)(4,1)}), s8[524288]{0:T(1024)(128)(4,1)S(1)}, s32[]{:S(2)}) async-start(s8[4718592]{0:T(1024)(128)(4,1)} %bitcast.181), calls=%async_computation.24 | async-start | bytes 1048576 | tf_op jit(solution)/shard_map/while
  763.4 7.0 copy-start.37
  770.3 5.6 copy-start.23
  770.3 5.6 copy-start.85
  775.9 12.0 copy-start.38
  776.7 11.2 copy-start.86
  776.7 13.6 %copy-start.77 = (bf16[3,768]{1,0:T(4,128)(2,1)S(1)}, bf16[3,768]{1,0:T(4,128)(2,1)}, u32[]{:S(2)}) copy-start(bf16[3,768]{1,0:T(4,128)(2,1)} %copy-done.76) | copy-start | bytes 13828 | tf_op jit(solution)/shard_map/while
  776.8 13.6 %copy-start.109 = (f32[2]{0:T(128)S(1)}, f32[2]{0:T(128)}, u32[]{:S(2)}) copy-start(f32[2]{0:T(128)} %copy-done.108) | copy-start | bytes 28 | tf_op jit(solution)/shard_map/while
  795.3 120.3 %reduce-scatter.11.cloned.1.call-start = ((), (), s32[]{:S(2)}) async-start(), calls=%async_computation.12 | async-start | bytes 2506752 | tf_op jit(solution)/shard_map/reduce_scatter | solution.py:284
  796.1 198.7 %reduce-scatter.13.cloned.1.call-start = ((), (), s32[]{:S(2)}) async-start(), calls=%async_computation.13 | async-start | bytes 5013504 | tf_op jit(solution)/shard_map/reduce_scatter | solution.py:285
  796.8 287.2 %reduce-scatter.17.cloned.1.call-start = ((), (), s32[]{:S(2)}) async-start(), calls=%async_computation.15 | async-start | bytes 6684672 | tf_op jit(solution)/shard_map/reduce_scatter | solution.py:287
  797.5 380.2 %reduce-scatter.9.cloned.1.call-start = ((), (), s32[]{:S(2)}) async-start(), calls=%async_computation.11 | async-start | bytes 7520256 | tf_op jit(solution)/shard_map/reduce_scatter | solution.py:283
  798.1 519.1 %reduce-scatter.15.cloned.1.call-start = ((), (), s32[]{:S(2)}) async-start(), calls=%async_computation.14 | async-start | bytes 13369344 | tf_op jit(solution)/shard_map/reduce_scatter | solution.py:286
  (63 other events, 130.4 us)
Sparse Core Ops, SparseCore 0:
  10.3 41.1 all-gather.7
  53.7 41.2 all-gather.13
  97.3 43.9 all-gather.11
  143.4 45.9 all-gather.5
  191.6 60.8 all-gather.9
  795.4 53.3 reduce-scatter.18
  853.7 61.9 reduce-scatter.10
  920.1 74.6 reduce-scatter.12
  999.8 84.2 reduce-scatter.16
  1088.5 89.2 reduce-scatter.8
  1182.9 134.2 reduce-scatter.14
where the time goes:
time: 1330 us; the launch traced here: 1320 us
  waiting for transfers between devices  924 us (69%)
  other arithmetic  126 us (9%)
  matrix products  112 us (8%)
  local copies, waits for them, and re-layouts  79.1 us (6%)
  blocking collectives  53.5 us (4%)
  between operations  14.2 us (1%)
    ppermute x4, waiting for transfers between devices, shifted(): return lax.ppermute(block, axis, route)  216 us
    reduce_scatter x1, waiting for transfers between devices, body(): lax.psum_scatter(in_total[None], 'dp', scatter_dimension=1, tiled=True)  140 us
    add x12, other arithmetic, step(): carry = tuple((a + b for a, b in zip(carry, grads)))  100 us
    reduce_scatter x1, waiting for transfers between devices, body(): lax.psum_scatter(qkv_total[None], 'dp', scatter_dimension=1, tiled=True)  93.7 us
    reduce_scatter x1, waiting for transfers between devices, body(): lax.psum_scatter(down_total[None], 'dp', scatter_dimension=1, tiled=True)  89.3 us
    dot_general x38, matrix products, product(): return jnp.dot(a, b, preferred_element_type=jnp.float32)  86.4 us
    reduce_scatter x1, waiting for transfers between devices, body(): lax.psum_scatter(cross_sum[None], 'dp', scatter_dimension=1, tiled=True)  79.1 us
    reduce_scatter x1, waiting for transfers between devices, body(): lax.psum_scatter(out_total[None], 'dp', scatter_dimension=1, tiled=True)  65.3 us
  transfers between devices with their start and end apart: 15, of which 14 were waited for; matrix products, arithmetic and copies ran while one was open for 1% of the time, Pallas kernels for 0%

commit v1 on v0

--- a/solution.py
+++ b/solution.py
@@ -3,6 +3,8 @@
 import jax
 import jax.numpy as jnp
 from jax import lax
+from jax.experimental import pallas as pl
+from jax.experimental.pallas import tpu as pltpu
 from jax.sharding import PartitionSpec as P
 
 HEADS = 12
@@ -231,6 +233,240 @@
     return lax.cond(flag, run_work, skip_work, operands)
 
 
+MESH = pl.DeviceIdType.MESH
+
+
+def ring_position(chip, chips):
+    return jnp.where(chip % 2 == 0, chip // 2, chips - 1 - chip // 2)
+
+
+def ring_chip(position, chips):
+    position = lax.rem(position + 2 * chips, chips)
+    return jnp.where(position < chips // 2, 2 * position, 2 * (chips - 1 - position) + 1)
+
+
+def ring_hops(index, chips):
+    long, short = chips // 2, chips - 1 - chips // 2
+    return (long, short) if index % 2 == 0 else (short, long)
+
+
+def entry_barrier(partners):
+    barrier = pltpu.get_barrier_semaphore()
+    for partner in partners:
+        pl.semaphore_signal(barrier, inc=1, device_id=partner, device_id_type=MESH)
+    pl.semaphore_wait(barrier, len(partners))
+
+
+def remote(src, dst, send_sem, recv_sem, target):
+    return pltpu.make_async_remote_copy(
+        src_ref=src,
+        dst_ref=dst,
+        send_sem=send_sem,
+        recv_sem=recv_sem,
+        device_id=target,
+        device_id_type=MESH,
+    )
+
+
+def gather_kernel(wide, count, *refs):
+    shards, fulls = refs[:count], refs[count : 2 * count]
+    own_sem, ring_send, ring_recv, twin_send, twin_recv = refs[2 * count :]
+    chips = wide // 2
+    section, me = lax.axis_index("section"), lax.axis_index("dp")
+    chip, core = me // 2, lax.rem(me, 2)
+    place = ring_position(chip, chips)
+    ahead = (section, 2 * ring_chip(place + 1, chips) + core)
+    behind = (section, 2 * ring_chip(place - 1, chips) + core)
+    twin = (section, 2 * chip + 1 - core)
+    entry_barrier((ahead, behind, twin))
+
+    def rows_of(index, origin_chip, origin_core):
+        rows = shards[index].shape[0]
+        start = pl.multiple_of((2 * origin_chip + origin_core) * rows, 16)
+        return fulls[index].at[pl.ds(start, rows)]
+
+    def ring_copy(index, way, hop):
+        origin = ring_chip(place - hop if way == 0 else place + hop, chips)
+        target = rows_of(index, origin, core)
+        source = shards[index] if hop == 0 else target
+        return remote(
+            source, target, ring_send.at[index, way, hop], ring_recv.at[index, way, hop], ahead if way == 0 else behind
+        )
+
+    def twin_copy(index, way, hop):
+        slot = 0 if hop == 0 else 1 + way * (chips // 2) + hop - 1
+        origin = ring_chip(place - hop if way == 0 else place + hop, chips)
+        target = rows_of(index, origin, core)
+        source = shards[index] if hop == 0 else target
+        return remote(source, target, twin_send.at[index, slot], twin_recv.at[index, slot], twin)
+
+    own = [pltpu.make_async_copy(shards[i], rows_of(i, chip, core), own_sem.at[i]) for i in range(count)]
+    for i in range(count):
+        for way in range(2):
+            ring_copy(i, way, 0).start()
+    for i in range(count):
+        twin_copy(i, 0, 0).start()
+        own[i].start()
+    for hop in range(chips // 2):
+        for i in range(count):
+            for way in range(2):
+                hops = ring_hops(i, chips)[way]
+                if hop < hops:
+                    ring_copy(i, way, hop).wait_recv()
+                    if hop + 1 < hops:
+                        ring_copy(i, way, hop + 1).start()
+                    twin_copy(i, way, hop + 1).start()
+    for i in range(count):
+        own[i].wait()
+        twin_copy(i, 0, 0).wait()
+        for way in range(2):
+            for hop in range(ring_hops(i, chips)[way]):
+                twin_copy(i, way, hop + 1).wait()
+                ring_copy(i, way, hop).wait_send()
+
+
+def gather_weights(wide, shards):
+    count, chips = len(shards), wide // 2
+    return pl.pallas_call(
+        partial(gather_kernel, wide, count),
+        out_shape=[jax.ShapeDtypeStruct((wide * s.shape[0], s.shape[1]), s.dtype) for s in shards],
+        in_specs=[pl.BlockSpec(memory_space=pl.ANY)] * count,
+        out_specs=[pl.BlockSpec(memory_space=pl.ANY)] * count,
+        scratch_shapes=[
+            pltpu.SemaphoreType.DMA((count,)),
+            pltpu.SemaphoreType.DMA((count, 2, chips // 2)),
+            pltpu.SemaphoreType.DMA((count, 2, chips // 2)),
+            pltpu.SemaphoreType.DMA((count, chips + 1)),
+            pltpu.SemaphoreType.DMA((count, chips + 1)),
+        ],
+        name="gather_weights",
+        compiler_params=pltpu.CompilerParams(collective_id=0, has_side_effects=True),
+    )(*shards)
+
+
+def reduce_kernel(wide, count, *refs):
+    grads, outs = refs[:count], refs[count : 2 * count]
+    blocks, twins, arrived = (refs[(2 + n) * count : (3 + n) * count] for n in range(3))
+    load_sem, twin_send, twin_recv, ring_send, ring_recv = refs[5 * count :]
+    chips = wide // 2
+    section, me = lax.axis_index("section"), lax.axis_index("dp")
+    chip, core = me // 2, lax.rem(me, 2)
+    place = ring_position(chip, chips)
+    ahead = (section, 2 * ring_chip(place + 1, chips) + core)
+    behind = (section, 2 * ring_chip(place - 1, chips) + core)
+    twin = (section, 2 * chip + 1 - core)
+    entry_barrier((ahead, behind, twin))
+
+    def offset_chip(way, distance):
+        return ring_chip(place + distance if way == 0 else place - distance, chips)
+
+    def rows_of(index, to_chip, to_core):
+        rows = outs[index].shape[0]
+        start = pl.multiple_of((2 * to_chip + to_core) * rows, 16)
+        return grads[index].at[pl.ds(start, rows)]
+
+    def twin_copy(index, way, distance):
+        slot = 0 if distance == 0 else 1 + way * (chips // 2) + distance - 1
+        return remote(
+            rows_of(index, offset_chip(way, distance), 1 - core),
+            twins[index].at[slot],
+            twin_send.at[index, slot],
+            twin_recv.at[index, slot],
+            twin,
+        )
+
+    def load_copy(index, way, distance):
+        slot = 0 if distance == 0 else 1 + way * (chips // 2) + distance - 1
+        return pltpu.make_async_copy(
+            rows_of(index, offset_chip(way, distance), core), blocks[index].at[slot], load_sem.at[index, slot]
+        )
+
+    def ring_copy(index, way, hop):
+        distance = ring_hops(index, chips)[way] - hop
+        slot = 1 + way * (chips // 2) + distance - 1
+        return remote(
+            blocks[index].at[slot],
+            arrived[index].at[way, hop],
+            ring_send.at[index, way, hop],
+            ring_recv.at[index, way, hop],
+            ahead if way == 0 else behind,
+        )
+
+    for hop in range(chips // 2 + 1):
+        for i in range(count):
+            for way in range(2):
+                distance = ring_hops(i, chips)[way] - hop
+                if distance > 0 or (distance == 0 and ring_hops(i, chips)[way] == chips // 2):
+                    twin_copy(i, way, distance).start()
+                    load_copy(i, way, distance).start()
+
+    def summed(terms, out):
+        @pl.loop(0, out.shape[0] // 16)
+        def _(group):
+            rows = pl.ds(pl.multiple_of(group * 16, 16), 16)
+            total = terms[0][rows].astype(jnp.float32)
+            for term in terms[1:]:
+                total += term[rows].astype(jnp.float32)
+            out[rows] = total.astype(out.dtype)
+
+    for hop in range(chips // 2):
+        for i in range(count):
+            for way in range(2):
+                hops = ring_hops(i, chips)[way]
+                distance = hops - hop
+                if distance <= 0:
+                    continue
+                slot = 1 + way * (chips // 2) + distance - 1
+                load_copy(i, way, distance).wait()
+                twin_copy(i, way, distance).wait_recv()
+                terms = [blocks[i].at[slot], twins[i].at[slot]]
+                if hop > 0:
+                    ring_copy(i, way, hop - 1).wait_recv()
+                    terms.append(arrived[i].at[way, hop - 1])
+                summed(terms, blocks[i].at[slot])
+                ring_copy(i, way, hop).start()
+    for i in range(count):
+        load_copy(i, 0, 0).wait()
+        twin_copy(i, 0, 0).wait_recv()
+        terms = [blocks[i].at[0], twins[i].at[0]]
+        for way in range(2):
+            hops = ring_hops(i, chips)[way]
+            ring_copy(i, way, hops - 1).wait_recv()
+            terms.append(arrived[i].at[way, hops - 1])
+        summed(terms, outs[i])
+    for i in range(count):
+        twin_copy(i, 0, 0).wait_send()
+        for way in range(2):
+            for hop in range(ring_hops(i, chips)[way]):
+                ring_copy(i, way, hop).wait_send()
+                twin_copy(i, way, hop + 1).wait_send()
+
+
+def reduce_grads(wide, grads):
+    count, chips = len(grads), wide // 2
+    shapes = [(g.shape[0] // wide, g.shape[1]) for g in grads]
+    return pl.pallas_call(
+        partial(reduce_kernel, wide, count),
+        out_shape=[jax.ShapeDtypeStruct(s, jnp.float32) for s in shapes],
+        in_specs=[pl.BlockSpec(memory_space=pl.ANY)] * count,
+        out_specs=[pl.BlockSpec(memory_space=pltpu.VMEM)] * count,
+        scratch_shapes=[pltpu.VMEM((chips + 1,) + s, jnp.bfloat16) for s in shapes]
+        + [pltpu.VMEM((chips + 1,) + s, jnp.bfloat16) for s in shapes]
+        + [pltpu.VMEM((2, chips // 2) + s, jnp.bfloat16) for s in shapes]
+        + [
+            pltpu.SemaphoreType.DMA((count, chips + 1)),
+            pltpu.SemaphoreType.DMA((count, chips + 1)),
+            pltpu.SemaphoreType.DMA((count, chips + 1)),
+            pltpu.SemaphoreType.DMA((count, 2, chips // 2)),
+            pltpu.SemaphoreType.DMA((count, 2, chips // 2)),
+        ],
+        name="reduce_grads",
+        compiler_params=pltpu.CompilerParams(
+            collective_id=1, has_side_effects=True, vmem_limit_bytes=60 * 2**20
+        ),
+    )(*grads)
+
+
 def body(
     block_in,
     cotangent,
@@ -247,15 +483,13 @@
     is_encoder = lax.axis_index("section") == 0
     is_decoder = jnp.logical_not(is_encoder)
     wide = lax.axis_size("dp")
-    gathered = (
-        lax.all_gather(gains, "dp", axis=2, tiled=True),
-        lax.all_gather(qkv_weight, "dp", axis=1, tiled=True),
-        lax.all_gather(out_weight, "dp", axis=1, tiled=True),
-        lax.all_gather(cross_weight, "dp", axis=1, tiled=True),
-        lax.all_gather(in_weight, "dp", axis=1, tiled=True),
-        lax.all_gather(down_weight, "dp", axis=1, tiled=True),
-    )
-    weights = tuple((w[0] for w in gathered))
+    tiled = all(w.shape[1] % 16 == 0 for w in (qkv_weight, out_weight, cross_weight, in_weight, down_weight))
+    shards = tuple((w[0] for w in (qkv_weight, out_weight, cross_weight, in_weight, down_weight)))
+    gains_full = lax.all_gather(gains[0], "dp", axis=1, tiled=True)
+    if tiled:
+        weights = (gains_full, *gather_weights(wide, shards))
+    else:
+        weights = (gains_full, *(lax.all_gather(s, "dp", axis=0, tiled=True) for s in shards))
     onehot = (sources[:, None] == jnp.arange(3, dtype=jnp.int32)[None, :]).astype(jnp.float32)
     counts = lax.psum(jnp.sum(onehot * lengths[:, None].astype(jnp.float32), axis=0), "dp")
     own_count = jnp.sum(onehot * counts[None, :], axis=1)
@@ -277,15 +511,12 @@
 
     start = tuple((jnp.zeros(w.shape, jnp.float32) for w in weights))
     carry, (outputs, input_grads) = lax.scan(step, start, (block_in[0], cotangent, lengths, scale))
-    gain_total, qkv_total, out_total, cross_sum, in_total, down_total = carry
-    reduced = (
-        lax.psum_scatter(gain_total[None], "dp", scatter_dimension=2, tiled=True),
-        lax.psum_scatter(qkv_total[None], "dp", scatter_dimension=1, tiled=True),
-        lax.psum_scatter(out_total[None], "dp", scatter_dimension=1, tiled=True),
-        lax.psum_scatter(cross_sum[None], "dp", scatter_dimension=1, tiled=True),
-        lax.psum_scatter(in_total[None], "dp", scatter_dimension=1, tiled=True),
-        lax.psum_scatter(down_total[None], "dp", scatter_dimension=1, tiled=True),
-    )
+    gains_reduced = lax.psum_scatter(carry[0], "dp", scatter_dimension=1, tiled=True)
+    if tiled:
+        sums = reduce_grads(wide, tuple((g.astype(jnp.bfloat16) for g in carry[1:])))
+    else:
+        sums = tuple((lax.psum_scatter(g, "dp", scatter_dimension=0, tiled=True) for g in carry[1:]))
+    reduced = (gains_reduced[None], *(g[None] for g in sums))
     return (
         outputs[None],
         input_grads[None],

time: 1330 us -> 829 us (0.62)
  waiting for transfers between devices: 924 us -> 217 us
  Pallas kernels: 0 us -> 173 us
  other arithmetic: 126 us -> 145 us
    reduce_scatter x5 -> x0, waiting for transfers between devices: 467 us -> none  [the longest x1 140 us: body(): lax.psum_scatter(in_total[None], 'dp', scatter_dimension=1, tiled=True)]
    all_gather x5 -> x0, waiting for transfers between devices: 184 us -> none  [the longest x1 63 us: body(): lax.all_gather(in_weight, 'dp', axis=1, tiled=True)]
    pallas_call x0 -> x2, Pallas kernels: none -> 173 us  [the longest x1 87.9 us: reduce_grads(): pl.pallas_call(partial(reduce_kernel, wide, count), out_shape=[jax.ShapeD...]
    unnamed x12 -> x2, waiting for transfers between devices: 56.4 us -> 0.04 us
    convert_element_type x0 -> x5, other arithmetic: none -> 19.4 us  [body(): g.astype(jnp.bfloat16)]
  transfers between devices with their start and end apart: 15 -> 5, of which waited for: 14 -> 4; matrix products, arithmetic and copies ran while one was open for 1% -> 3% of each run, Pallas kernels for 0% -> 11%
where the time goes in v1:
time: 829 us; the launch traced here: 825 us
  waiting for transfers between devices  217 us (26%)
  Pallas kernels  173 us (21%)
  other arithmetic  145 us (17%)
  matrix products  113 us (14%)
  local copies, waits for them, and re-layouts  90.2 us (11%)
  blocking collectives  53.2 us (6%)
  between operations  14.4 us (2%)
  loops' own time  12.7 us (2%)
    ppermute x4, waiting for transfers between devices, shifted(): return lax.ppermute(block, axis, route)  217 us
    add x12, other arithmetic, step(): carry = tuple((a + b for a, b in zip(carry, grads)))  100 us
    dot_general x38, matrix products, product(): return jnp.dot(a, b, preferred_element_type=jnp.float32)  88.1 us
    pallas_call x1, Pallas kernels, reduce_grads(): pl.pallas_call(partial(reduce_kernel, wide, count), out_shape=[jax.ShapeD...  87.9 us
    pallas_call x1, Pallas kernels, gather_weights(): pl.pallas_call(partial(gather_kernel, wide, count), out_shape=[jax.ShapeD...  85.2 us
    another operation x18, local copies, waits for them, and re-layouts  39.9 us
    psum x1, blocking collectives, body(): lax.psum(jnp.sum(onehot * lengths[:, None].astype(jnp.float32), axis=0),...  34.9 us
    convert_element_type x5, other arithmetic, body(): g.astype(jnp.bfloat16)  19.4 us
  transfers between devices with their start and end apart: 5, of which 4 were waited for; matrix products, arithmetic and copies ran while one was open for 3% of the time, Pallas kernels for 11%

profile of v1, /device:TPU:0, one launch (start us, length us, event | category | flops | bytes accessed | tf_op | source)
XLA Modules:
  0.0 824.6 jit_solution(16490150378091491796)
XLA Ops:
  9.4 34.9 %psum.7 = f32[3]{0:T(128)S(1)} all-reduce(f32[3]{0:T(128)S(1)} %select_reduce_fusion.1), channel_id=1, replica_groups=mesh['section'=2,'dp'=16] {'dp'}, use_global_device_ids=true, to_apply=%region_2.0 | all-reduce | flops 3 | bytes 24 | tf_op jit(solution)/shard_map/psum | solution.py:494
  45.0 18.2 %all-gather = bf16[1,3,768]{1,0,2:T(2,128)(2,1)S(1)} all-gather(bf16[1,3,48]{1,0,2:T(2,128)(2,1)S(1)} %copy.180), channel_id=2, replica_groups=mesh['section'=2,'dp'=16] {'dp'}, dimensions={2}, use_global_device_ids=true | all-gather | bytes 4896 | tf_op jit(solution)/shard_map/all_gather | solution.py:488
  64.5 85.2 %gather_weights.1 = (bf16[768,2304]{1,0:T(8,128)(2,1)}, bf16[768,768]{1,0:T(8,128)(2,1)}, bf16[768,1536]{1,0:T(8,128)(2,1)}, bf16[768,4096]{1,0:T(8,128)(2,1)}, bf16[2048,768]{1,0:T(8,128)(2,1)}) custom-call(bf16[48,2304]{1,0:T(8,128)(2,1)} %bitcast.236, bf16[48,768]{1,0:T(8,128)(2,1)} %bitcast.240, bf16[48,1536]{1,0:T(8,128)(2,1)} %bitcast.239, ...), custom_call_target="tpu_custom_call" | custom-call | tf_op jit(solution)/shard_map/gather_weights/pallas_call | solution.py:330
  149.6 547.2 %while.25 = (s32[]{:T(128)}, f32[3,768]{1,0:T(4,128)}, f32[768,2304]{1,0:T(8,128)}, f32[768,768]{1,0:T(8,128)}, f32[768,1536]{1,0:T(8,128)}, /*index=5*/f32[768,...) while((s32[]{:T(128)}, f32[3,768]{1,0:T(4,128)}, ...), condition=%wide.region_43.44_spmd.clone, body=%wide.region_4.43_spmd.clone.sunk | while | flops 31191597056 | bytes 995691712 | solution.py:513
  150.9 19.1 %conditional.9 = (bf16[256,1536]{1,0:T(8,128)(2,1)}, bf16[256,768]{1,0:T(8,128)(2,1)}) conditional(s32[]{:T(128)} %convert_element_type.465, () %tuple.115, (bf16[256,768]{1,0:T(8,128)(2,1)S(1)}, bf16[3,768]{1,0:T(4,128)(2,1)S(1)}, bf16[768,2304]{1,0:T(8,128)(2,1)}, bf16[768,768]{1,0:T(8,128)(2,1)}, bf16[768,4096]{1,0:T(8,128)(2,1)}, ...), branch_computations={%region_5.5_spmd, %region_6.11_spmd} | conditional | flops 4443474944 | bytes 91417240 | solution.py:233
  151.1 3.1 convolution_convert_fusion
  155.6 4.0 fusion.170
  159.6 2.4 fusion.15
  167.4 2.7 convolution_convert_fusion.1
  172.8 17.5 %collective-permute-done = bf16[256,1536]{0,1:T(8,128)(2,1)S(1)} collective-permute-done((bf16[256,1536]{0,1:T(8,128)(2,1)S(1)}, bf16[256,1536]{0,1:T(8,128)(2,1)S(1)}, u32[]{:S(2)}, u32[]{:S(2)}) %collective-permute-start) | collective-permute-done | bytes 786464 | tf_op jit(solution)/shard_map/while/body/eval_jaxpr/ppermute | solution.py:21
  190.4 22.9 %conditional.10 = (bf16[256,768]{1,0:T(8,128)(2,1)}, f32[256,768]{1,0:T(8,128)}, bf16[256,1536]{0,1:T(8,128)(2,1)}, f32[3,768]{1,0:T(4,128)}, f32[768,2304]{1,0:...) conditional(s32[]{:T(128)} %convert_element_type.464, ...), branch_computations={%region_12.12_spmd, %region_13.28_spmd} | conditional | flops 13973643264 | bytes 421253344 | solution.py:233
  195.1 2.7 broadcast.339.clone
  197.9 3.0 broadcast.341
  200.9 3.3 broadcast.337
  204.2 6.1 broadcast.340
  216.0 2.0 bitcast_dynamic-update-slice_fusion.4
  217.9 92.3 %collective-permute-done.1 = bf16[256,1536]{1,0:T(8,128)(2,1)S(1)} collective-permute-done((bf16[256,1536]{1,0:T(8,128)(2,1)S(1)}, bf16[256,1536]{1,0:T(8,128)(2,1)S(1)}, u32[]{:S(2)}, u32[]{:S(2)}) %collective-permute-start.1) | collective-permute-done | bytes 786464 | tf_op jit(solution)/shard_map/while/body/eval_jaxpr/ppermute | solution.py:21
  310.2 59.6 %conditional.11 = (f32[256,768]{1,0:T(8,128)}, f32[3,768]{1,0:T(4,128)}, f32[768,2304]{1,0:T(8,128)}, f32[768,768]{1,0:T(8,128)}, f32[768,1536]{1,0:T(8,128)}, /*index=5*/f32[768,4096]{1,0:T(8,128)}, f32[2048,768]{1,0:T(8,128)}) conditional(s32[]{:T(128)} %convert_element_type.465, () %tuple.118, (bf16[256,768]{1,0:T(8,128)(2,1)S(1)}, ...), branch_computations={%region_29.29_spmd, %region_30.42_spmd} | conditional | flops 12748716032 | bytes 285084384 | solution.py:233
  312.2 3.1 convolution_convert_fusion.6
  331.7 2.5 fusion.122
  334.2 2.0 multiply_reduce_fusion.15
  352.0 3.2 fusion.150
  355.2 3.8 fusion.156
  359.0 4.1 fusion.148
  363.1 6.5 fusion.129
  369.8 8.4 %select_add_fusion.17 = f32[2048,768]{1,0:T(8,128)} fusion(f32[2048,768]{1,0:T(8,128)} %get-tuple-element.781, f32[2048,768]{1,0:T(8,128)} %get-tuple-element.710, f32[2048,768]{1,0:T(8,128)} %get-tuple-element.711, pred[]{:T(512)S(6)} %compare.3), kind=kLoop, calls=%fused_computation.272.clone.1 | loop fusion | flops 4718592 | bytes 25165824 | tf_op jit(solution)/shard_map/while/body/eval_jaxpr/add | solution.py:509
  378.2 15.9 %select_add_fusion.16 = f32[768,4096]{1,0:T(8,128)} fusion(f32[768,4096]{1,0:T(8,128)} %get-tuple-element.780, f32[768,4096]{1,0:T(8,128)} %get-tuple-element.708, f32[768,4096]{1,0:T(8,128)} %get-tuple-element.709, pred[]{:T(512)S(6)} %compare.3), kind=kLoop, calls=%fused_computation.270.clone.1 | loop fusion | flops 9437184 | bytes 50331648 | tf_op jit(solution)/shard_map/while/body/eval_jaxpr/add | solution.py:509
  394.2 6.9 select_add_fusion.15
  401.2 5.6 select_add_fusion.14
  407.6 9.2 %select_add_fusion.13 = f32[768,2304]{1,0:T(8,128)} fusion(f32[768,2304]{1,0:T(8,128)} %get-tuple-element.777, f32[768,2304]{1,0:T(8,128)} %get-tuple-element.702, f32[768,2304]{1,0:T(8,128)} %get-tuple-element.703, pred[]{:T(512)S(6)} %compare.3), kind=kLoop, calls=%fused_computation.271.clone.1 | loop fusion | flops 5308416 | bytes 28311552 | tf_op jit(solution)/shard_map/while/body/eval_jaxpr/add | solution.py:509
  416.8 2.3 bitcast_dynamic-update-slice_fusion.5
  420.6 19.1 %conditional.9 = (bf16[256,1536]{1,0:T(8,128)(2,1)}, bf16[256,768]{1,0:T(8,128)(2,1)}) conditional(s32[]{:T(128)} %convert_element_type.465, () %tuple.115, (bf16[256,768]{1,0:T(8,128)(2,1)S(1)}, bf16[3,768]{1,0:T(4,128)(2,1)S(1)}, bf16[768,2304]{1,0:T(8,128)(2,1)}, bf16[768,768]{1,0:T(8,128)(2,1)}, bf16[768,4096]{1,0:T(8,128)(2,1)}, ...), branch_computations={%region_5.5_spmd, %region_6.11_spmd} | conditional | flops 4443474944 | bytes 91417240 | solution.py:233
  420.9 3.1 convolution_convert_fusion
  425.4 4.0 fusion.170
  429.3 2.4 fusion.15
  437.1 2.7 convolution_convert_fusion.1
  442.5 16.4 %collective-permute-done = bf16[256,1536]{0,1:T(8,128)(2,1)S(1)} collective-permute-done((bf16[256,1536]{0,1:T(8,128)(2,1)S(1)}, bf16[256,1536]{0,1:T(8,128)(2,1)S(1)}, u32[]{:S(2)}, u32[]{:S(2)}) %collective-permute-start) | collective-permute-done | bytes 786464 | tf_op jit(solution)/shard_map/while/body/eval_jaxpr/ppermute | solution.py:21
  459.0 22.8 %conditional.10 = (bf16[256,768]{1,0:T(8,128)(2,1)}, f32[256,768]{1,0:T(8,128)}, bf16[256,1536]{0,1:T(8,128)(2,1)}, f32[3,768]{1,0:T(4,128)}, f32[768,2304]{1,0:...) conditional(s32[]{:T(128)} %convert_element_type.464, ...), branch_computations={%region_12.12_spmd, %region_13.28_spmd} | conditional | flops 13973643264 | bytes 421253344 | solution.py:233
  463.7 2.7 broadcast.339.clone
  466.5 3.0 broadcast.341
  469.5 3.3 broadcast.337
  472.8 6.1 broadcast.340
  486.5 91.0 %collective-permute-done.1 = bf16[256,1536]{1,0:T(8,128)(2,1)S(1)} collective-permute-done((bf16[256,1536]{1,0:T(8,128)(2,1)S(1)}, bf16[256,1536]{1,0:T(8,128)(2,1)S(1)}, u32[]{:S(2)}, u32[]{:S(2)}) %collective-permute-start.1) | collective-permute-done | bytes 786464 | tf_op jit(solution)/shard_map/while/body/eval_jaxpr/ppermute | solution.py:21
  577.4 59.6 %conditional.11 = (f32[256,768]{1,0:T(8,128)}, f32[3,768]{1,0:T(4,128)}, f32[768,2304]{1,0:T(8,128)}, f32[768,768]{1,0:T(8,128)}, f32[768,1536]{1,0:T(8,128)}, /*index=5*/f32[768,4096]{1,0:T(8,128)}, f32[2048,768]{1,0:T(8,128)}) conditional(s32[]{:T(128)} %convert_element_type.465, () %tuple.118, (bf16[256,768]{1,0:T(8,128)(2,1)S(1)}, ...), branch_computations={%region_29.29_spmd, %region_30.42_spmd} | conditional | flops 12748716032 | bytes 285084384 | solution.py:233
  579.1 3.1 convolution_convert_fusion.6
  598.6 2.8 fusion.122
  601.5 2.0 multiply_reduce_fusion.15
  619.2 3.2 fusion.150
  622.5 3.7 fusion.156
  626.2 4.1 fusion.148
  630.3 6.5 fusion.129
  637.0 10.2 %select_add_fusion.17 = f32[2048,768]{1,0:T(8,128)} fusion(f32[2048,768]{1,0:T(8,128)} %get-tuple-element.781, f32[2048,768]{1,0:T(8,128)} %get-tuple-element.710, f32[2048,768]{1,0:T(8,128)} %get-tuple-element.711, pred[]{:T(512)S(6)} %compare.3), kind=kLoop, calls=%fused_computation.272.clone.1 | loop fusion | flops 4718592 | bytes 25165824 | tf_op jit(solution)/shard_map/while/body/eval_jaxpr/add | solution.py:509
  647.2 18.6 %select_add_fusion.16 = f32[768,4096]{1,0:T(8,128)} fusion(f32[768,4096]{1,0:T(8,128)} %get-tuple-element.780, f32[768,4096]{1,0:T(8,128)} %get-tuple-element.708, f32[768,4096]{1,0:T(8,128)} %get-tuple-element.709, pred[]{:T(512)S(6)} %compare.3), kind=kLoop, calls=%fused_computation.270.clone.1 | loop fusion | flops 9437184 | bytes 50331648 | tf_op jit(solution)/shard_map/while/body/eval_jaxpr/add | solution.py:509
  665.9 6.9 select_add_fusion.15
  672.9 5.6 select_add_fusion.14
  679.3 11.2 %select_add_fusion.13 = f32[768,2304]{1,0:T(8,128)} fusion(f32[768,2304]{1,0:T(8,128)} %get-tuple-element.777, f32[768,2304]{1,0:T(8,128)} %get-tuple-element.702, f32[768,2304]{1,0:T(8,128)} %get-tuple-element.703, pred[]{:T(512)S(6)} %compare.3), kind=kLoop, calls=%fused_computation.271.clone.1 | loop fusion | flops 5308416 | bytes 28311552 | tf_op jit(solution)/shard_map/while/body/eval_jaxpr/add | solution.py:509
  690.6 2.3 bitcast_dynamic-update-slice_fusion.5
  698.5 2.8 convert_element_type.287.refs_1_
  701.3 4.2 convert_element_type.288.refs_2_
  706.4 2.0 convert_element_type.290.refs_4_
  709.9 2.2 convert_element_type.286.refs_0_
  712.1 8.2 convert_element_type.289.refs_3_
  720.3 87.9 %reduce_grads.1 = (f32[48,2304]{1,0:T(8,128)}, f32[48,768]{1,0:T(8,128)}, f32[48,1536]{1,0:T(8,128)}, f32[48,4096]{1,0:T(8,128)}, f32[128,768]{1,0:T(8,128)}) custom-call(bf16[768,2304]{1,0:T(8,128)(2,1)} %convert_element_type.286.refs_0_, bf16[768,768]{1,0:T(8,128)(2,1)} %convert_element_type.287.refs_1_, bf16[768,1536]{1,0:T(8,128)(2,1)} %convert_element_type.288.refs_2_, ...), custom_call_target="tpu_custom_call" | custom-call | tf_op jit(solution)/shard_map/reduce_grads/pallas_call | solution.py:448
  814.7 2.1 copy.277
  (383 shorter events, 121.9 us)
Async XLA Ops:
  7.2 801.0 %reduce-scatter.4.cloned.1.call-start = ((), (), s32[]{:S(2)}) async-start(), calls=%async_computation.1 | async-start | bytes 417792
  149.8 40.5 %copy-start.109 = (f32[2]{0:T(128)}, f32[2]{0:T(128)S(1)}, u32[]{:S(2)}) copy-start(f32[2]{0:T(128)S(1)} %get-tuple-element.818) | copy-start | bytes 28 | tf_op jit(solution)/shard_map/while
  149.8 160.4 %copy-start.77 = (bf16[3,768]{1,0:T(4,128)(2,1)}, bf16[3,768]{1,0:T(4,128)(2,1)S(1)}, u32[]{:S(2)}) copy-start(bf16[3,768]{1,0:T(4,128)(2,1)S(1)} %get-tuple-element.810) | copy-start | bytes 13828 | tf_op jit(solution)/shard_map/while
  150.9 39.5 %copy-start.108 = (s32[2]{0:T(128)S(1)}, s32[2]{0:T(128)}, u32[]{:S(2)}) copy-start(s32[2]{0:T(128)} %get-tuple-element.816) | copy-start | bytes 28 | tf_op jit(solution)/shard_map/while
  155.6 7.0 slice-start
  159.6 3.5 slice-start.1
  171.5 18.9 %collective-permute-start = (bf16[256,1536]{0,1:T(8,128)(2,1)S(1)}, bf16[256,1536]{0,1:T(8,128)(2,1)S(1)}, u32[]{:S(2)}, u32[]{:S(2)}) collective-permute-start(bf16[256,1536]{0,1:T(8,128)(2,1)S(1)} %copy.202), channel_id=1, source_target_pairs={{0,16},{1,17},{2,18},{3,19},{4,20},{5,21},{6,22},{7,23},{8,24},{9,... | collective-permute-start | bytes 2359304 | tf_op jit(solution)/shard_map/while/body/eval_jaxpr/ppermute | solution.py:21
  214.7 95.5 %collective-permute-start.1 = (bf16[256,1536]{1,0:T(8,128)(2,1)S(1)}, bf16[256,1536]{1,0:T(8,128)(2,1)S(1)}, u32[]{:S(2)}, u32[]{:S(2)}) collective-permute-start(bf16[256,1536]{1,0:T(8,128)(2,1)S(1)} %copy.203), channel_id=1, source_target_pairs={{16,0},{17,1},{18,2},{19,3},{20,4},{21,5},{22,6},{23,7},{24,8},{25... | collective-permute-start | bytes 2359304 | tf_op jit(solution)/shard_map/while/body/eval_jaxpr/ppermute | solution.py:21
  311.3 4.1 copy-start.89
  320.0 3.2 slice-start.4
  323.1 13.7 %copy-start.8 = (f32[256,768]{1,0:T(8,128)}, f32[256,768]{1,0:T(8,128)S(1)}, u32[]{:S(2)}) copy-start(f32[256,768]{1,0:T(8,128)S(1)} %get-tuple-element.545) | copy-start | bytes 2359300 | tf_op jit(solution)/shard_map/while/body/eval_jaxpr/cond
  327.4 3.4 copy-start.25
  328.5 3.2 copy-start.27
  331.7 5.2 copy-start.22
  341.2 3.7 copy-start.36
  341.2 3.7 copy-start.51
  341.2 3.7 copy-start.75
  352.0 3.2 copy-start.23
  352.0 3.2 copy-start.26
  359.0 4.1 copy-start.9
  359.0 4.1 copy-start.66
  359.0 4.1 copy-start.68
  378.2 15.9 %slice-start.8 = ((s8[4718592]{0:T(1024)(128)(4,1)}), s8[4194304]{0:T(1024)(128)(4,1)S(1)}, s32[]{:S(2)}) async-start(s8[4718592]{0:T(1024)(128)(4,1)} %bitcast.176), calls=%async_computation.10 | async-start | bytes 8388608 | tf_op jit(solution)/shard_map/while
  378.2 15.9 %slice-start.9 = ((s8[4718592]{0:T(1024)(128)(4,1)}), s8[524288]{0:T(1024)(128)(4,1)S(1)}, s32[]{:S(2)}) async-start(s8[4718592]{0:T(1024)(128)(4,1)} %bitcast.176), calls=%async_computation.11 | async-start | bytes 1048576 | tf_op jit(solution)/shard_map/while
  394.2 7.0 copy-start.38
  401.1 5.6 copy-start.24
  401.2 5.6 copy-start.85
  406.8 10.1 %copy-start.39 = (f32[768,768]{1,0:T(8,128)}, f32[768,768]{1,0:T(8,128)S(1)}, u32[]{:S(2)}) copy-start(f32[768,768]{1,0:T(8,128)S(1)} %select_add_fusion.14) | copy-start | bytes 7077892 | tf_op jit(solution)/shard_map/while
  407.6 9.2 %copy-start.86 = (f32[3,768]{1,0:T(4,128)}, f32[3,768]{1,0:T(4,128)S(1)}, u32[]{:S(2)}) copy-start(f32[3,768]{1,0:T(4,128)S(1)} %select_add_fusion.12) | copy-start | bytes 27652 | tf_op jit(solution)/shard_map/while
  407.6 11.6 %copy-start.78 = (bf16[3,768]{1,0:T(4,128)(2,1)S(1)}, bf16[3,768]{1,0:T(4,128)(2,1)}, u32[]{:S(2)}) copy-start(bf16[3,768]{1,0:T(4,128)(2,1)} %copy-done.77) | copy-start | bytes 13828 | tf_op jit(solution)/shard_map/while
  407.6 11.5 %copy-start.110 = (f32[2]{0:T(128)S(1)}, f32[2]{0:T(128)}, u32[]{:S(2)}) copy-start(f32[2]{0:T(128)} %copy-done.109) | copy-start | bytes 28 | tf_op jit(solution)/shard_map/while
  419.6 39.4 %copy-start.109 = (f32[2]{0:T(128)}, f32[2]{0:T(128)S(1)}, u32[]{:S(2)}) copy-start(f32[2]{0:T(128)S(1)} %get-tuple-element.818) | copy-start | bytes 28 | tf_op jit(solution)/shard_map/while
  419.6 157.9 %copy-start.77 = (bf16[3,768]{1,0:T(4,128)(2,1)}, bf16[3,768]{1,0:T(4,128)(2,1)S(1)}, u32[]{:S(2)}) copy-start(bf16[3,768]{1,0:T(4,128)(2,1)S(1)} %get-tuple-element.810) | copy-start | bytes 13828 | tf_op jit(solution)/shard_map/while
  420.6 38.3 %copy-start.108 = (s32[2]{0:T(128)S(1)}, s32[2]{0:T(128)}, u32[]{:S(2)}) copy-start(s32[2]{0:T(128)} %get-tuple-element.816) | copy-start | bytes 28 | tf_op jit(solution)/shard_map/while
  425.4 7.0 slice-start
  429.3 3.5 slice-start.1
  441.2 17.8 %collective-permute-start = (bf16[256,1536]{0,1:T(8,128)(2,1)S(1)}, bf16[256,1536]{0,1:T(8,128)(2,1)S(1)}, u32[]{:S(2)}, u32[]{:S(2)}) collective-permute-start(bf16[256,1536]{0,1:T(8,128)(2,1)S(1)} %copy.202), channel_id=1, source_target_pairs={{0,16},{1,17},{2,18},{3,19},{4,20},{5,21},{6,22},{7,23},{8,24},{9,... | collective-permute-start | bytes 2359304 | tf_op jit(solution)/shard_map/while/body/eval_jaxpr/ppermute | solution.py:21
  483.2 94.2 %collective-permute-start.1 = (bf16[256,1536]{1,0:T(8,128)(2,1)S(1)}, bf16[256,1536]{1,0:T(8,128)(2,1)S(1)}, u32[]{:S(2)}, u32[]{:S(2)}) collective-permute-start(bf16[256,1536]{1,0:T(8,128)(2,1)S(1)} %copy.203), channel_id=1, source_target_pairs={{16,0},{17,1},{18,2},{19,3},{20,4},{21,5},{22,6},{23,7},{24,8},{25... | collective-permute-start | bytes 2359304 | tf_op jit(solution)/shard_map/while/body/eval_jaxpr/ppermute | solution.py:21
  578.3 4.1 copy-start.89
  590.1 14.0 %copy-start.8 = (f32[256,768]{1,0:T(8,128)}, f32[256,768]{1,0:T(8,128)S(1)}, u32[]{:S(2)}) copy-start(f32[256,768]{1,0:T(8,128)S(1)} %get-tuple-element.545) | copy-start | bytes 2359300 | tf_op jit(solution)/shard_map/while/body/eval_jaxpr/cond
  594.3 3.4 copy-start.25
  595.4 3.2 copy-start.27
  598.6 5.5 copy-start.22
  608.4 3.7 copy-start.36
  608.4 3.7 copy-start.51
  608.4 3.7 copy-start.75
  619.2 3.2 copy-start.23
  619.2 3.2 copy-start.26
  626.2 4.1 copy-start.9
  626.2 4.1 copy-start.66
  626.2 4.1 copy-start.68
  647.2 18.6 %slice-start.8 = ((s8[4718592]{0:T(1024)(128)(4,1)}), s8[4194304]{0:T(1024)(128)(4,1)S(1)}, s32[]{:S(2)}) async-start(s8[4718592]{0:T(1024)(128)(4,1)} %bitcast.176), calls=%async_computation.10 | async-start | bytes 8388608 | tf_op jit(solution)/shard_map/while
  647.2 18.6 %slice-start.9 = ((s8[4718592]{0:T(1024)(128)(4,1)}), s8[524288]{0:T(1024)(128)(4,1)S(1)}, s32[]{:S(2)}) async-start(s8[4718592]{0:T(1024)(128)(4,1)} %bitcast.176), calls=%async_computation.11 | async-start | bytes 1048576 | tf_op jit(solution)/shard_map/while
  665.9 7.0 copy-start.38
  672.8 5.6 copy-start.24
  672.9 5.6 copy-start.85
  678.5 12.1 %copy-start.39 = (f32[768,768]{1,0:T(8,128)}, f32[768,768]{1,0:T(8,128)S(1)}, u32[]{:S(2)}) copy-start(f32[768,768]{1,0:T(8,128)S(1)} %select_add_fusion.14) | copy-start | bytes 7077892 | tf_op jit(solution)/shard_map/while
  679.3 11.2 %copy-start.86 = (f32[3,768]{1,0:T(4,128)}, f32[3,768]{1,0:T(4,128)S(1)}, u32[]{:S(2)}) copy-start(f32[3,768]{1,0:T(4,128)S(1)} %select_add_fusion.12) | copy-start | bytes 27652 | tf_op jit(solution)/shard_map/while
  679.3 13.6 %copy-start.78 = (bf16[3,768]{1,0:T(4,128)(2,1)S(1)}, bf16[3,768]{1,0:T(4,128)(2,1)}, u32[]{:S(2)}) copy-start(bf16[3,768]{1,0:T(4,128)(2,1)} %copy-done.77) | copy-start | bytes 13828 | tf_op jit(solution)/shard_map/while
  679.3 13.6 %copy-start.110 = (f32[2]{0:T(128)S(1)}, f32[2]{0:T(128)}, u32[]{:S(2)}) copy-start(f32[2]{0:T(128)} %copy-done.109) | copy-start | bytes 28 | tf_op jit(solution)/shard_map/while
  701.3 5.1 copy-start.21
  701.3 7.1 slice-start.6
  706.4 3.5 slice-start.7
  808.2 8.6 %copy-start.93 = (f32[128,768]{1,0:T(8,128)S(1)}, f32[128,768]{1,0:T(8,128)}, u32[]{:S(2)}) copy-start(f32[128,768]{1,0:T(8,128)} %get-tuple-element.309) | copy-start | bytes 1179652
  (55 other events, 104.7 us)
Sparse Core Ops, SparseCore 0:
  698.6 54.2 reduce-scatter.3

commit v2 on v0

v2 whole, which is shorter than its diff:
```python
from functools import partial

import jax
import jax.numpy as jnp
from jax import lax
from jax.experimental import pallas as pl
from jax.experimental.pallas import tpu as pltpu
from jax.sharding import PartitionSpec as P

HEADS = 12
HEAD_DIM = 64


EPS = 1e-06
NEG = -1000000000.0


MESH = pl.DeviceIdType.MESH
VMEM_LIMIT = 62 * 2**20
F32, BF16 = jnp.float32, jnp.bfloat16
ANY = pl.BlockSpec(memory_space=pl.ANY)
SMEM = pl.BlockSpec(memory_space=pltpu.SMEM)
VMEM = pl.BlockSpec(memory_space=pltpu.VMEM)


def ring_position(chip, chips):
    return jnp.where(chip % 2 == 0, chip // 2, chips - 1 - chip // 2)


def ring_chip(position, chips):
    position = lax.rem(position + 2 * chips, chips)
    return jnp.where(position < chips // 2, 2 * position, 2 * (chips - 1 - position) + 1)


def ring_hops(long_way, chips):
    long, short = chips // 2, chips - 1 - chips // 2
    return (long, short) if long_way == 0 else (short, long)


def slot_of(way, distance, chips):
    return 0 if distance == 0 else 1 + way * (chips // 2) + distance - 1


def entry_barrier(partners):
    barrier = pltpu.get_barrier_semaphore()
    for partner in partners:
        pl.semaphore_signal(barrier, inc=1, device_id=partner, device_id_type=MESH)
    pl.semaphore_wait(barrier, len(partners))


def remote(src, dst, send_sem, recv_sem, target):
    return pltpu.make_async_remote_copy(
        src_ref=src,
        dst_ref=dst,
        send_sem=send_sem,
        recv_sem=recv_sem,
        device_id=target,
        device_id_type=MESH,
    )


class Place:
    def __init__(self, wide):
        self.chips = wide // 2
        self.section, self.me = lax.axis_index("section"), lax.axis_index("dp")
        self.chip, self.core = self.me // 2, lax.rem(self.me, 2)
        self.spot = ring_position(self.chip, self.chips)
        self.ahead = (self.section, 2 * ring_chip(self.spot + 1, self.chips) + self.core)
        self.behind = (self.section, 2 * ring_chip(self.spot - 1, self.chips) + self.core)
        self.twin = (self.section, 2 * self.chip + 1 - self.core)
        self.across = (1 - self.section, self.me)

    def next_of(self, way):
        return self.ahead if way == 0 else self.behind

    def chip_at(self, way, distance):
        return ring_chip(self.spot + distance if way == 0 else self.spot - distance, self.chips)


def block_rows(ref, rows, chip, core):
    return ref.at[pl.ds(pl.multiple_of((2 * chip + core) * rows, rows), rows)]


class Gather:
    def __init__(self, place, names, shards, fulls, rows, long_way, sems):
        self.place, self.names = place, names
        self.shards, self.fulls, self.rows, self.long_way = shards, fulls, rows, long_way
        self.own_sem, self.ring_send, self.ring_recv, self.twin_send, self.twin_recv = sems

    def hops(self, name, way):
        return ring_hops(self.long_way[name], self.place.chips)[way]

    def pieces(self, name, way, hop):
        at = self.place
        origin = at.chip_at(way, -hop)
        target = block_rows(self.fulls[name], self.rows[name], origin, at.core)
        own = self.shards.get(name)
        return (own if hop == 0 and own is not None else target), target

    def ring(self, name, way, hop):
        source, target = self.pieces(name, way, hop)
        i = self.names.index(name)
        return remote(
            source, target, self.ring_send.at[i, way, hop], self.ring_recv.at[i, way, hop], self.place.next_of(way)
        )

    def pair(self, name, way, hop):
        source, target = self.pieces(name, way, hop)
        i, slot = self.names.index(name), slot_of(way, hop, self.place.chips)
        return remote(source, target, self.twin_send.at[i, slot], self.twin_recv.at[i, slot], self.place.twin)

    def own(self, name):
        source, target = self.pieces(name, 0, 0)
        return pltpu.make_async_copy(source, target, self.own_sem.at[self.names.index(name)])

    def start(self, name):
        for way in range(2):
            self.ring(name, way, 0).start()
        self.pair(name, 0, 0).start()
        if name in self.shards:
            self.own(name).start()

    def step(self, name, hop):
        for way in range(2):
            hops = self.hops(name, way)
            if hop < hops:
                self.ring(name, way, hop).wait_recv()
                if hop + 1 < hops:
                    self.ring(name, way, hop + 1).start()
                self.pair(name, way, hop + 1).start()

    def complete(self, name):
        if name in self.shards:
            self.own(name).wait()
        self.pair(name, 0, 0).wait_recv()
        for way in range(2):
            for hop in range(self.hops(name, way)):
                self.pair(name, way, hop + 1).wait_recv()

    def drain(self):
        for name in self.names:
            if name not in self.all_names:
                continue
            self.pair(name, 0, 0).wait_send()
            for way in range(2):
                for hop in range(self.hops(name, way)):
                    self.pair(name, way, hop + 1).wait_send()
                    self.ring(name, way, hop).wait_send()


GATHER_NAMES = ("gains", "counts", "qkv", "out", "crossE", "crossD", "in", "down")
LONG_WAY = {"gains": 0, "counts": 1, "qkv": 0, "out": 1, "crossE": 0, "crossD": 1, "in": 1, "down": 0}


def gather_kernel(wide, *refs):
    ins, outs, sems = refs[:7], refs[7:15], refs[15:]
    shards = dict(zip(("gains", "counts", "qkv", "out", "cross", "in", "down"), ins))
    fulls = dict(zip(GATHER_NAMES, outs))
    rows = {n: outs[i].shape[0] // wide for i, n in enumerate(GATHER_NAMES)}
    at = Place(wide)
    across_send, across_recv = sems[5], sems[6]
    entry_barrier((at.ahead, at.behind, at.twin, at.across))
    passed = remote(
        shards["cross"],
        block_rows(fulls["crossE"], rows["crossE"], at.chip, at.core),
        across_send,
        across_recv,
        at.across,
    )

    def run(names, own):
        gather = Gather(at, GATHER_NAMES, own, fulls, rows, LONG_WAY, sems[:5])
        gather.all_names = names
        for name in names:
            if name == "crossE":
                passed.wait_recv()
            gather.start(name)
        for hop in range(at.chips // 2):
            for name in names:
                gather.step(name, hop)
        for name in names:
            gather.complete(name)
        gather.drain()

    @pl.when(at.section == 0)
    def _():
        passed.start()
        names = ("gains", "counts", "qkv", "out", "in", "down")
        run(names, {n: shards[n] for n in names})
        passed.wait_send()

    @pl.when(at.section == 1)
    def _():
        names = ("gains", "counts", "qkv", "out", "crossD", "in", "down", "crossE")
        own = {n: shards[n] for n in names if n in shards}
        own["crossD"] = shards["cross"]
        run(names, own)


def gather_sems(count, chips):
    return [
        pltpu.SemaphoreType.DMA((count,)),
        pltpu.SemaphoreType.DMA((count, 2, chips // 2)),
        pltpu.SemaphoreType.DMA((count, 2, chips // 2)),
        pltpu.SemaphoreType.DMA((count, chips + 1)),
        pltpu.SemaphoreType.DMA((count, chips + 1)),
        pltpu.SemaphoreType.DMA,
        pltpu.SemaphoreType.DMA,
    ]


def gather_weights(wide, gains, counts, qkv, out, cross, inner, down):
    shards = (gains, counts, qkv, out, cross, inner, down)
    fulls = (gains, counts, qkv, out, cross, cross, inner, down)
    return pl.pallas_call(
        partial(gather_kernel, wide),
        out_shape=[jax.ShapeDtypeStruct((wide * s.shape[0], s.shape[1]), s.dtype) for s in fulls],
        in_specs=[ANY] * len(shards),
        out_specs=[ANY] * len(fulls),
        scratch_shapes=gather_sems(len(fulls), wide // 2),
        name="gather_weights",
        compiler_params=pltpu.CompilerParams(collective_id=0, has_side_effects=True),
    )(*shards)


class Scatter:
    def __init__(self, place, names, grads, rows, long_way, blocks, twins, arrived, sems):
        self.place, self.names, self.grads, self.rows, self.long_way = place, names, grads, rows, long_way
        self.blocks, self.twins, self.arrived = blocks, twins, arrived
        self.load_sem, self.twin_send, self.twin_recv, self.ring_send, self.ring_recv = sems

    def hops(self, name, way):
        return ring_hops(self.long_way[name], self.place.chips)[way]

    def pair(self, name, way, distance):
        at, i = self.place, self.names.index(name)
        slot = slot_of(way, distance, at.chips)
        source = block_rows(self.grads[name], self.rows[name], at.chip_at(way, distance), 1 - at.core)
        return remote(source, self.twins[name].at[slot], self.twin_send.at[i, slot], self.twin_recv.at[i, slot], at.twin)

    def load(self, name, way, distance):
        at, i = self.place, self.names.index(name)
        slot = slot_of(way, distance, at.chips)
        source = block_rows(self.grads[name], self.rows[name], at.chip_at(way, distance), at.core)
        return pltpu.make_async_copy(source, self.blocks[name].at[slot], self.load_sem.at[i, slot])

    def ring(self, name, way, hop):
        at, i = self.place, self.names.index(name)
        slot = slot_of(way, self.hops(name, way) - hop, at.chips)
        return remote(
            self.blocks[name].at[slot],
            self.arrived[name].at[way, hop],
            self.ring_send.at[i, way, hop],
            self.ring_recv.at[i, way, hop],
            at.next_of(way),
        )

    def slots(self, name):
        found = []
        for hop in range(self.place.chips // 2 + 1):
            for way in range(2):
                distance = self.hops(name, way) - hop
                if distance > 0 or (distance == 0 and way == self.long_way[name]):
                    found.append((way, distance))
        return found

    def start(self, name):
        for way, distance in self.slots(name):
            self.pair(name, way, distance).start()
            self.load(name, way, distance).start()

    def add(self, terms, out):
        group = 16 if out.shape[0] % 16 == 0 else out.shape[0]

        @pl.loop(0, out.shape[0] // group)
        def _(n):
            rows = pl.ds(pl.multiple_of(n * group, group), group)
            total = terms[0][rows].astype(F32)
            for term in terms[1:]:
                total += term[rows].astype(F32)
            out[rows] = total.astype(out.dtype)

    def step(self, name, way, hop):
        distance = self.hops(name, way) - hop
        if distance <= 0:
            return
        slot = slot_of(way, distance, self.place.chips)
        self.load(name, way, distance).wait()
        self.pair(name, way, distance).wait_recv()
        terms = [self.blocks[name].at[slot], self.twins[name].at[slot]]
        if hop > 0:
            self.ring(name, way, hop - 1).wait_recv()
            terms.append(self.arrived[name].at[way, hop - 1])
        self.add(terms, self.blocks[name].at[slot])
        self.ring(name, way, hop).start()

    def finish(self, name, out):
        self.load(name, self.long_way[name], 0).wait()
        self.pair(name, self.long_way[name], 0).wait_recv()
        terms = [self.blocks[name].at[0], self.twins[name].at[0]]
        for way in range(2):
            last = self.hops(name, way) - 1
            self.ring(name, way, last).wait_recv()
            terms.append(self.arrived[name].at[way, last])
        self.add(terms, out)

    def drain(self, name):
        for way, distance in self.slots(name):
            self.pair(name, way, distance).wait_send()
        for way in range(2):
            for hop in range(self.hops(name, way)):
                self.ring(name, way, hop).wait_send()


SCATTER_NAMES = ("down", "in", "crossD", "crossE", "out", "qkv", "gains")


def reduce_kernel(wide, *refs):
    count = len(SCATTER_NAMES)
    grads = dict(zip(SCATTER_NAMES, refs[:count]))
    outs = dict(zip(("down", "in", "cross", "out", "qkv", "gains"), refs[count : 2 * count - 1]))
    refs = refs[2 * count - 1 :]
    blocks, twins, arrived = (dict(zip(SCATTER_NAMES, refs[n * count : (n + 1) * count])) for n in range(3))
    passed_out, passed_in = refs[3 * count : 3 * count + 2]
    sems = refs[3 * count + 2 :]
    rows = {n: grads[n].shape[0] // wide for n in SCATTER_NAMES}
    at = Place(wide)
    entry_barrier((at.ahead, at.behind, at.twin, at.across))
    passed = remote(passed_out, passed_in, sems[5], sems[6], at.across)

    def run(names, results):
        scatter = Scatter(at, SCATTER_NAMES, grads, rows, LONG_WAY, blocks, twins, arrived, sems[:5])
        for name in names:
            scatter.start(name)
        for hop in range(at.chips // 2):
            for name in names:
                for way in range(2):
                    scatter.step(name, way, hop)
        for name in names:
            scatter.finish(name, results[name])
            if name == "crossE":
                passed.start()
        for name in names:
            scatter.drain(name)

    @pl.when(at.section == 0)
    def _():
        run(("down", "in", "out", "qkv", "gains"), outs)
        passed.wait_recv()
        outs["cross"][...] = passed_in[...]

    @pl.when(at.section == 1)
    def _():
        run(("crossE", "down", "in", "crossD", "out", "qkv", "gains"), {**outs, "crossD": outs["cross"], "crossE": passed_out})
        passed.wait_send()


def scatter_scratch(shapes, dtypes, chips):
    return (
        [pltpu.VMEM((chips + 1,) + s, d) for s, d in zip(shapes, dtypes)]
        + [pltpu.VMEM((chips + 1,) + s, d) for s, d in zip(shapes, dtypes)]
        + [pltpu.VMEM((2, chips // 2) + s, d) for s, d in zip(shapes, dtypes)]
    )


def scatter_sems(count, chips):
    return [
        pltpu.SemaphoreType.DMA((count, chips + 1)),
        pltpu.SemaphoreType.DMA((count, chips + 1)),
        pltpu.SemaphoreType.DMA((count, chips + 1)),
        pltpu.SemaphoreType.DMA((count, 2, chips // 2)),
        pltpu.SemaphoreType.DMA((count, 2, chips // 2)),
        pltpu.SemaphoreType.DMA,
        pltpu.SemaphoreType.DMA,
    ]


def reduce_grads(wide, grads):
    chips = wide // 2
    shapes = [(grads[n].shape[0] // wide, grads[n].shape[1]) for n in SCATTER_NAMES]
    dtypes = [grads[n].dtype for n in SCATTER_NAMES]
    of = dict(zip(SCATTER_NAMES, shapes))
    outs = [of["down"], of["in"], of["crossD"], of["out"], of["qkv"], of["gains"]]
    return pl.pallas_call(
        partial(reduce_kernel, wide),
        out_shape=[jax.ShapeDtypeStruct(s, F32) for s in outs],
        in_specs=[ANY] * len(shapes),
        out_specs=[VMEM] * len(outs),
        scratch_shapes=scatter_scratch(shapes, dtypes, chips)
        + [pltpu.VMEM(of["crossE"], F32), pltpu.VMEM(of["crossE"], F32)]
        + scatter_sems(len(shapes), chips),
        name="reduce_grads",
        compiler_params=pltpu.CompilerParams(collective_id=1, has_side_effects=True, vmem_limit_bytes=VMEM_LIMIT),
    )(*(grads[n] for n in SCATTER_NAMES))


def dot(a, b, over_a=1, over_b=0):
    return lax.dot_general(a, b, (((over_a,), (over_b,)), ((), ())), preferred_element_type=F32)


def span(start, size):
    return pl.ds(pl.multiple_of(start, size), size)


def each(total, tile, work):
    @pl.loop(0, total // tile)
    def _(n):
        work(span(n * tile, tile))


ROWS = 64


def norm_into(h_ref, gain, out_ref):
    def work(at):
        h = h_ref[at].astype(F32)
        inv_root = lax.rsqrt(jnp.mean(h * h, axis=-1, keepdims=True) + EPS)
        out_ref[at] = (h * inv_root * gain).astype(out_ref.dtype)

    each(h_ref.shape[0], ROWS, work)


def norm_back(dn_ref, h_ref, gain, gain_sum, row, finish):
    gain_sum[row] = jnp.zeros(gain_sum.shape[1:], F32)

    def work(at):
        h, dn = h_ref[at].astype(F32), dn_ref[at].astype(F32)
        inv_root = lax.rsqrt(jnp.mean(h * h, axis=-1, keepdims=True) + EPS)
        scaled = h * inv_root
        product = dn * scaled
        gain_sum[row] += jnp.sum(product.reshape(-1, 8, product.shape[1]), axis=0)
        inner = dn * gain
        finish(at, inv_root * (inner - scaled * jnp.mean(product * gain, axis=-1, keepdims=True)))

    each(h_ref.shape[0], ROWS, work)


def pair_columns(ref, rows, start, two):
    return ref[rows, span(start + two * 2 * HEAD_DIM, 2 * HEAD_DIM)]


def side_masks():
    lane = lax.broadcasted_iota(jnp.int32, (1, 2 * HEAD_DIM), 1)
    first = lane < HEAD_DIM
    return first, (first.astype(F32).astype(BF16), (1 - first.astype(F32)).astype(BF16))


def masked_scores(q, k, seq, length):
    scores = dot(q, k, 1, 1) * HEAD_DIM ** (-0.5)
    if length is not None:
        query = lax.broadcasted_iota(jnp.int32, (seq, seq), 0)
        key = lax.broadcasted_iota(jnp.int32, (seq, seq), 1)
        scores = jnp.where((key <= query) & (key < length), scores, NEG)
    return scores


def softmax(scores):
    expo = jnp.exp(scores - jnp.max(scores, axis=-1, keepdims=True))
    return expo * (1.0 / jnp.sum(expo, axis=-1, keepdims=True))


def attend(q_ref, q_at, k_ref, k_at, v_ref, v_at, out_ref, seq, lengths, probs_ref=None):
    pairs = q_ref.shape[0] // seq
    first, keeps = side_masks()

    @pl.loop(0, pairs * (HEADS // 2))
    def _(n):
        pair, two = n // (HEADS // 2), lax.rem(n, HEADS // 2)
        rows = span(pair * seq, seq)
        length = None if lengths is None else lengths[pair]
        q, k, v = (pair_columns(r, rows, a, two) for r, a in ((q_ref, q_at), (k_ref, k_at), (v_ref, v_at)))
        halves = []
        for side in range(2):
            probs = softmax(masked_scores(q * keeps[side], k, seq, length)).astype(BF16)
            if probs_ref is not None:
                probs_ref[2 * n + side] = probs
            halves.append(dot(probs, v))
        out_ref[rows, span(two * 2 * HEAD_DIM, 2 * HEAD_DIM)] = jnp.where(first, *halves).astype(BF16)


def attend_back(q_ref, q_at, k_ref, k_at, v_ref, v_at, do_ref, dq, dk, dv, seq, lengths, probs_ref=None):
    pairs = q_ref.shape[0] // seq
    first, keeps = side_masks()

    @pl.loop(0, pairs * (HEADS // 2))
    def _(n):
        pair, two = n // (HEADS // 2), lax.rem(n, HEADS // 2)
        rows = span(pair * seq, seq)
        length = None if lengths is None else lengths[pair]
        q, k, v = (pair_columns(r, rows, a, two) for r, a in ((q_ref, q_at), (k_ref, k_at), (v_ref, v_at)))
        d_out = pair_columns(do_ref, rows, 0, two)
        sides = []
        for side in range(2):
            if probs_ref is None:
                probs = softmax(masked_scores(q * keeps[side], k, seq, length))
                probs_low = probs.astype(BF16)
            else:
                probs_low = probs_ref[2 * n + side]
                probs = probs_low.astype(F32)
            d_probs = dot(d_out * keeps[side], v, 1, 1)
            centre = jnp.sum(probs * d_probs, axis=-1, keepdims=True)
            d_scores = (probs * (d_probs - centre)).astype(BF16)
            sides.append((dot(d_scores, k), dot(d_scores, q, 0, 0), dot(probs_low, d_out, 0, 0)))
        for (ref, start), both, factor in zip((dq, dk, dv), zip(*sides), (HEAD_DIM ** (-0.5), HEAD_DIM ** (-0.5), 1.0)):
            ref[rows, span(start + two * 2 * HEAD_DIM, 2 * HEAD_DIM)] = (jnp.where(first, *both) * factor).astype(BF16)


def gelu_parts(gate):
    root, cubic = 0.7978845608028654, 0.044715
    square = gate * gate
    bent = jnp.tanh(root * gate * (1.0 + cubic * square))
    half = 0.5 * (1.0 + bent)
    slope = half + 0.5 * gate * (1.0 - bent * bent) * root * (1.0 + 3.0 * cubic * square)
    return gate * half, slope


FF_TILE = 512


def mlp_forward(a_ref, w_in, w_down, into_ref, hidden_ref=None, slopes_ref=None):
    ff = w_in.shape[1] // 2

    @pl.loop(0, ff // FF_TILE)
    def _(n):
        gates, uppers = span(n * FF_TILE, FF_TILE), span(ff + n * FF_TILE, FF_TILE)
        gate, upper = dot(a_ref[...], w_in[:, gates]), dot(a_ref[...], w_in[:, uppers])
        active, slope = gelu_parts(gate)
        hidden = (active * upper).astype(BF16)
        if hidden_ref is not None:
            hidden_ref[:, gates] = hidden
            slopes_ref[:, gates] = (slope * upper).astype(BF16)
            slopes_ref[:, uppers] = active.astype(BF16)
        if w_down is not None:
            into_ref[...] += dot(hidden, w_down[gates, :])


def mlp_back(d_low, w_in, w_down, slopes_ref, dn_ref):
    ff = w_in.shape[1] // 2
    dn_ref[...] = jnp.zeros(dn_ref.shape, F32)

    @pl.loop(0, ff // FF_TILE)
    def _(n):
        gates, uppers = span(n * FF_TILE, FF_TILE), span(ff + n * FF_TILE, FF_TILE)
        d_hidden = dot(d_low[...], w_down[gates, :], 1, 1)
        d_gate = (d_hidden * slopes_ref[:, gates]).astype(BF16)
        d_upper = (d_hidden * slopes_ref[:, uppers]).astype(BF16)
        slopes_ref[:, gates], slopes_ref[:, uppers] = d_gate, d_upper
        dn_ref[...] += dot(d_gate, w_in[:, gates], 1, 1) + dot(d_upper, w_in[:, uppers], 1, 1)


def product_into(a_ref, w_ref, out_ref, tile, w_at=0, transposed=False):
    width = out_ref.shape[1]

    @pl.loop(0, width // tile)
    def _(n):
        if transposed:
            value = dot(a_ref[...], w_ref[span(w_at + n * tile, tile), :], 1, 1)
        else:
            value = dot(a_ref[...], w_ref[:, span(w_at + n * tile, tile)])
        out_ref[:, span(n * tile, tile)] = value.astype(out_ref.dtype)


def add_product(base_ref, a_ref, w, out_ref):
    out_ref[...] = base_ref[...].astype(F32) + dot(a_ref[...], w)


class Moves:
    def __init__(self, sems):
        self.sems, self.used = sems, 0

    def start(self, src, dst):
        copy = pltpu.make_async_copy(src, dst, self.sems.at[self.used])
        self.used += 1
        copy.start()
        return copy


def weight_grad(moves, a_ref, y_ref, grad_hbm, tile_rows, tile_columns, column_at=0):
    depth, width = a_ref.shape[1], y_ref.shape[1]

    def inner(stage):
        copies = []
        for i in range(depth // tile_rows):
            for j in range(width // tile_columns):
                n = len(copies)
                if n >= 2:
                    copies[n - 2].wait()
                rows, columns = pl.ds(i * tile_rows, tile_rows), pl.ds(j * tile_columns, tile_columns)
                stage[n % 2] = dot(a_ref[:, rows], y_ref[:, columns], 0, 0).astype(BF16)
                goal = grad_hbm.at[rows, pl.ds(column_at + j * tile_columns, tile_columns)]
                copies.append(moves.start(stage.at[n % 2], goal))
        for copy in copies[-2:]:
            copy.wait()

    pl.run_scoped(inner, pltpu.VMEM((2, tile_rows, tile_columns), BF16))


def forward_kernel(
    seq, lengths, x_in, gains_in, w_qkv_in, w_out_in, w_in_in, w_down_in,
    joined_out, attended_out, middle_out, final_out, memory_out, landed,
    w_qkv, w_out, w_in, w_down, x, gains, normed, joined, attended, middle, load_sem, send_sem, recv_sem,
):
    section, me = lax.axis_index("section"), lax.axis_index("dp")
    across = (1 - section, me)
    entry_barrier((across,))
    pairs = x.shape[0] // seq
    moves = Moves(load_sem)
    loads = [moves.start(a, b) for a, b in ((x_in, x), (gains_in, gains), (w_qkv_in, w_qkv), (w_out_in, w_out))]

    def to_dec(pair):
        rows = pl.ds(pair * seq, seq)
        return remote(memory_out.at[rows], landed.at[rows], send_sem.at[pair], recv_sem.at[pair], across)

    def attention(lengths):
        loads[0].wait()
        loads[1].wait()
        norm_into(x, gains[0:1], normed)
        loads[2].wait()
        product_into(normed, w_qkv, joined, 768)
        width = x.shape[1]
        attend(joined, 0, joined, width, joined, 2 * width, attended, seq, lengths)
        loads[3].wait()
        add_product(x, attended, w_out[...], middle)
        return [moves.start(a, b) for a, b in ((joined, joined_out), (attended, attended_out), (middle, middle_out))]

    @pl.when(section == 0)
    def _():
        later = [moves.start(a, b) for a, b in ((w_in_in, w_in), (w_down_in, w_down))]
        stores = attention(None)
        norm_into(middle, gains[1:2], normed)
        for copy in later + stores[2:]:
            copy.wait()
        mlp_forward(normed, w_in, w_down, middle)
        stores.append(moves.start(middle, final_out))
        norm_into(middle, gains[2:3], normed)
        store = moves.start(normed, memory_out)
        store.wait()
        for pair in range(pairs):
            to_dec(pair).start()
        for copy in stores[:2] + stores[3:]:
            copy.wait()
        for pair in range(pairs):
            to_dec(pair).wait_send()

    @pl.when(section == 1)
    def _():
        for copy in attention(lengths):
            copy.wait()
        for pair in range(pairs):
            to_dec(pair).wait_recv()


def forward(x, lengths, gains, w_qkv, w_out, w_in, w_down, seq):
    rows, width = x.shape
    vmem = pltpu.VMEM
    return pl.pallas_call(
        partial(forward_kernel, seq),
        out_shape=[
            jax.ShapeDtypeStruct((rows, w_qkv.shape[1]), BF16),
            jax.ShapeDtypeStruct((rows, width), BF16),
            jax.ShapeDtypeStruct((rows, width), F32),
            jax.ShapeDtypeStruct((rows, width), F32),
            jax.ShapeDtypeStruct((rows, width), BF16),
            jax.ShapeDtypeStruct((rows, width), BF16),
        ],
        in_specs=[SMEM] + [ANY] * 6,
        out_specs=[ANY] * 6,
        scratch_shapes=[vmem(w.shape, BF16) for w in (w_qkv, w_out, w_in, w_down)]
        + [
            vmem((rows, width), BF16),
            vmem(gains.shape, F32),
            vmem((rows, width), BF16),
            vmem((rows, w_qkv.shape[1]), BF16),
            vmem((rows, width), BF16),
            vmem((rows, width), F32),
            pltpu.SemaphoreType.DMA((16,)),
            pltpu.SemaphoreType.DMA((rows // seq,)),
            pltpu.SemaphoreType.DMA((rows // seq,)),
        ],
        name="forward",
        compiler_params=pltpu.CompilerParams(collective_id=2, has_side_effects=True, vmem_limit_bytes=VMEM_LIMIT),
    )(lengths, x, gains, w_qkv, w_out, w_in, w_down)


def backward_kernel(
    seq, lengths, factors, x_in, gains_in, cot_in, joined_in, attended_in, middle_in, final_in, memory_in, landed,
    w_qkv_in, w_out_in, w_enc_in, w_dec_in, w_in_in, w_down_in,
    block_out, input_out, gains_out, g_down, g_in, g_dec, g_enc, g_out, g_qkv, returned,
    gains, gain_sum, back, load_sem, send_sem, recv_sem,
):
    section, me = lax.axis_index("section"), lax.axis_index("dp")
    across = (1 - section, me)
    entry_barrier((across,))
    rows, width = x_in.shape
    pairs = rows // seq
    moves = Moves(load_sem)
    vmem = pltpu.VMEM
    wide = vmem((rows, width), F32)
    slim = vmem((rows, width), BF16)
    copy = moves.start(gains_in, gains)
    copy.wait()

    def to_enc(pair):
        at = pl.ds(pair * seq, seq)
        return remote(back.at[at], returned.at[at], send_sem.at[pair], recv_sem.at[pair], across)

    def self_back(lengths, d_middle, x, normed, d_low, w_qkv, w_out, joined, attended, d_attended, dn, row):
        each(rows, ROWS, lambda at: d_low.__setitem__(at, d_middle[at].astype(BF16)))
        weight_grad(moves, attended, d_low, g_out, 768, 768)
        product_into(d_low, w_out, d_attended, 768, transposed=True)
        attend_back(
            joined, 0, joined, width, joined, 2 * width, d_attended,
            (joined, 0), (joined, width), (joined, 2 * width), seq, lengths,
        )
        weight_grad(moves, normed, joined, g_qkv, 768, 768)
        product_into(joined, w_qkv, dn, 768, transposed=True)

        def finish(at, d_input):
            d_middle[at] = d_middle[at] + d_input

        norm_back(dn, x, gains[row : row + 1], gain_sum, row, finish)
        store = moves.start(d_middle, input_out)
        store.wait()

    def encoder(w_qkv, w_out, w_in, w_down, x, joined, attended, middle, final, normed, hidden, slopes, d_low, d_attended, dn, d_memory):
        loads = [
            moves.start(a, b)
            for a, b in (
                (middle_in, middle), (w_in_in, w_in), (final_in, final), (w_down_in, w_down), (x_in, x),
                (joined_in, joined), (attended_in, attended), (w_out_in, w_out), (w_qkv_in, w_qkv), (memory_in, block_out),
            )
        ]
        for load in loads:
            load.wait()
        norm_into(middle, gains[1:2], normed)
        mlp_forward(normed, w_in, None, None, hidden, slopes)
        for pair in range(pairs):
            to_enc(pair).wait_recv()
        load = moves.start(returned, d_memory)
        load.wait()

        def finish_final(at, d_input):
            final[at] = d_input
            d_low[at] = d_input.astype(BF16)

        norm_back(d_memory, final, gains[2:3], gain_sum, 2, finish_final)
        weight_grad(moves, hidden, d_low, g_down, 1024, 768)
        mlp_back(d_low, w_in, w_down, slopes, dn)
        weight_grad(moves, normed, slopes, g_in, 768, 1024)

        def finish_middle(at, d_input):
            final[at] = final[at] + d_input

        norm_back(dn, middle, gains[1:2], gain_sum, 1, finish_middle)
        norm_into(x, gains[0:1], normed)
        self_back(None, final, x, normed, d_low, w_qkv, w_out, joined, attended, d_attended, dn, 0)

    @pl.when(section == 0)
    def _():
        ff = w_down_in.shape[0]
        pl.run_scoped(
            encoder,
            vmem(w_qkv_in.shape, BF16), vmem(w_out_in.shape, BF16), vmem(w_in_in.shape, BF16), vmem(w_down_in.shape, BF16),
            slim, vmem((rows, 3 * width), BF16), slim, wide, wide, slim,
            vmem((rows, ff), BF16), vmem((rows, 2 * ff), BF16), slim, slim, wide, slim,
        )

    def middle_part(w_enc, w_dec, w_in, w_down, memory, cot, normed_a, queries, keyval, probs, crossed, after, normed_b, slopes, hidden, d_low, dn, d_low2, d_crossed, middle):
        loads = [
            moves.start(a, b)
            for a, b in (
                (middle_in, middle), (w_dec_in, w_dec), (landed, memory), (w_enc_in, w_enc),
                (w_in_in, w_in), (w_down_in, w_down), (cot_in, cot),
            )
        ]
        loads[0].wait()
        norm_into(middle, gains[1:2], normed_a)
        loads[1].wait()
        product_into(normed_a, w_dec, queries, 768)
        loads[2].wait()
        loads[3].wait()
        product_into(memory, w_enc, keyval, 768)
        attend(queries, 0, keyval, 0, keyval, width, crossed, seq, None, probs)
        add_product(middle, crossed, w_dec[:, width:], after)
        norm_into(after, gains[2:3], normed_b)
        for load in loads[4:]:
            load.wait()
        final = dn
        final[...] = after[...]
        mlp_forward(normed_b, w_in, w_down, final, hidden, slopes)

        @pl.loop(0, pairs * (seq // ROWS))
        def _(n):
            pair, group = n // (seq // ROWS), lax.rem(n, seq // ROWS)
            at = span(n * ROWS, ROWS)
            position = group * ROWS + lax.broadcasted_iota(jnp.int32, (ROWS, 1), 0)
            d_low2[at] = final[at].astype(BF16)
            d_final = jnp.where(position < lengths[pair], cot[at].astype(F32) * factors[pair], 0.0)
            dn[at] = d_final
            d_low[at] = d_final.astype(BF16)

        store = moves.start(d_low2, block_out)
        d_after = middle_grad = None
        return store

    def decoder_middle(w_enc, w_dec, w_in, w_down, memory, cot, normed_a, queries, keyval, probs, crossed, after, normed_b, slopes, hidden, d_low, dn, d_low2, d_crossed, middle, d_after):
        store = middle_part(w_enc, w_dec, w_in, w_down, memory, cot, normed_a, queries, keyval, probs, crossed, after, normed_b, slopes, hidden, d_low, dn, d_low2, d_crossed, middle)
        d_after[...] = dn[...]
        mlp_back(d_low, w_in, w_down, slopes, dn)
        store.wait()

        def finish_after(at, d_input):
            total = d_after[at] + d_input
            d_after[at] = total
            d_low2[at] = total.astype(BF16)

        norm_back(dn, after, gains[2:3], gain_sum, 2, finish_after)
        @pl.loop(0, 1)
        def _(n):
            d_crossed[...] = dot(d_low2[...], w_dec[:, width:], 1, 1).astype(BF16)

        d_queries, d_keyval = cot, keyval
        attend_back(
            queries, 0, keyval, 0, keyval, width, d_crossed, (d_queries, 0), (d_keyval, 0), (d_keyval, width), seq, None, probs
        )
        for pair in range(pairs):
            at = pl.ds(pair * seq, seq)
            back[at] = dot(d_keyval[at], w_enc[...], 1, 1).astype(BF16)
            to_enc(pair).start()
        @pl.loop(0, 1)
        def _(n):
            dn[...] = dot(d_queries[...], w_dec[:, :width], 1, 1)

        def finish_middle(at, d_input):
            d_after[at] = d_after[at] + d_input

        norm_back(dn, middle, gains[1:2], gain_sum, 1, finish_middle)
        weight_grad(moves, hidden, d_low, g_down, 1024, 768)
        weight_grad(moves, normed_b, slopes, g_in, 768, 1024)
        weight_grad(moves, normed_a, d_queries, g_dec, 768, 768)
        weight_grad(moves, crossed, d_low2, g_dec, 768, 768, column_at=width)
        weight_grad(moves, memory, d_keyval, g_enc, 768, 768)

    def decoder(d_after):
        ff = w_down_in.shape[0]
        pl.run_scoped(
            lambda *refs: decoder_middle(*refs, d_after),
            vmem(w_enc_in.shape, BF16), vmem(w_dec_in.shape, BF16), vmem(w_in_in.shape, BF16), vmem(w_down_in.shape, BF16),
            slim, slim, slim, slim, vmem((rows, 2 * width), BF16), vmem((pairs * HEADS, seq, seq), BF16), slim, wide, slim,
            vmem((rows, 2 * ff), BF16), vmem((rows, ff), BF16), slim, wide, slim, slim, wide,
        )

        def front(w_qkv, w_out, x, joined, attended, normed, d_low, d_attended, dn):
            loads = [
                moves.start(a, b)
                for a, b in ((x_in, x), (attended_in, attended), (w_out_in, w_out), (joined_in, joined), (w_qkv_in, w_qkv))
            ]
            for load in loads:
                load.wait()
            norm_into(x, gains[0:1], normed)
            self_back(lengths, d_after, x, normed, d_low, w_qkv, w_out, joined, attended, d_attended, dn, 0)

        pl.run_scoped(
            front,
            vmem(w_qkv_in.shape, BF16), vmem(w_out_in.shape, BF16),
            slim, vmem((rows, 3 * width), BF16), slim, slim, slim, slim, wide,
        )
        for pair in range(pairs):
            to_enc(pair).wait_send()

    @pl.when(section == 1)
    def _():
        pl.run_scoped(decoder, wide)

    for row in range(3):
        gains_out[row : row + 1] = jnp.sum(gain_sum[row], axis=0, keepdims=True)


def backward(seq, lengths, factors, x, gains, cot, saved, landed, weights):
    joined, attended, middle, final, memory = saved
    w_qkv, w_out, w_enc, w_dec, w_in, w_down = weights
    rows, width = x.shape
    args = (lengths, factors, x, gains, cot, joined, attended, middle, final, memory, landed, *weights)
    shaped = jax.ShapeDtypeStruct
    return pl.pallas_call(
        partial(backward_kernel, seq),
        out_shape=[shaped((rows, width), BF16), shaped((rows, width), F32), shaped(gains.shape, F32)]
        + [shaped(w.shape, BF16) for w in (w_down, w_in, w_dec, w_enc, w_out, w_qkv)]
        + [shaped((rows, width), BF16)],
        in_specs=[SMEM] * 2 + [ANY] * (len(args) - 2),
        out_specs=[ANY, ANY, VMEM] + [ANY] * 7,
        scratch_shapes=[
            pltpu.VMEM(gains.shape, F32),
            pltpu.VMEM((3, 8, width), F32),
            pltpu.VMEM((rows, width), BF16),
            pltpu.SemaphoreType.DMA((64,)),
            pltpu.SemaphoreType.DMA((rows // seq,)),
            pltpu.SemaphoreType.DMA((rows // seq,)),
        ],
        name="backward",
        compiler_params=pltpu.CompilerParams(collective_id=3, has_side_effects=True, vmem_limit_bytes=VMEM_LIMIT),
    )(*args)


def shifted(block, axis, distance):
    devices = range(lax.axis_size(axis))
    route = [(i - distance, i) for i in devices if i - distance in devices]
    return lax.ppermute(block, axis, route)


def plain_product(a, b):
    return jnp.dot(a, b, preferred_element_type=jnp.float32)


def plain_split_heads(v):
    return v.reshape(v.shape[0], HEADS, -1)


def plain_norm_forward(h, norm_gain):
    inv_root = lax.rsqrt(jnp.mean(h * h, axis=-1, keepdims=True) + EPS)
    return (h * inv_root * norm_gain.astype(jnp.float32), inv_root)


def plain_norm_back(d_normed, h, inv_root, norm_gain):
    scaled = h * inv_root
    d_gain = jnp.sum(d_normed * scaled, axis=0)
    inner = d_normed * norm_gain.astype(jnp.float32)
    d_input = inv_root * (inner - scaled * jnp.mean(inner * scaled, axis=-1, keepdims=True))
    return (d_input, d_gain)


def plain_score_block(q, k, key_mask):
    scores = jnp.einsum(
        "qhd,khd->hqk", plain_split_heads(q), plain_split_heads(k), preferred_element_type=jnp.float32
    ) * HEAD_DIM ** (-0.5)
    if key_mask is not None:
        scores = jnp.where(key_mask[None], scores, NEG)
    return scores


def plain_attend_forward(q, k, v, key_mask):
    scores = plain_score_block(q, k, key_mask)
    highest = jnp.max(scores, axis=-1, keepdims=True)
    expo = jnp.exp(scores - highest)
    total = jnp.sum(expo, axis=-1, keepdims=True)
    weights = (expo / total).astype(jnp.bfloat16)
    output = jnp.einsum("hqk,khd->qhd", weights, plain_split_heads(v), preferred_element_type=jnp.float32)
    return (output.reshape(q.shape[0], -1), highest + jnp.log(total))


def plain_attend_back(q, k, v, key_mask, log_total, d_out):
    scores = plain_score_block(q, k, key_mask)
    probs = jnp.exp(scores - log_total)
    heads_dout = plain_split_heads(d_out)
    d_value = jnp.einsum(
        "hqk,qhd->khd", probs.astype(jnp.bfloat16), heads_dout, preferred_element_type=jnp.float32
    )
    d_probs = jnp.einsum(
        "qhd,khd->hqk", heads_dout, plain_split_heads(v), preferred_element_type=jnp.float32
    )
    centre = jnp.sum(probs * d_probs, axis=-1, keepdims=True)
    d_scores = (probs * (d_probs - centre)).astype(jnp.bfloat16)
    d_query = jnp.einsum(
        "hqk,khd->qhd", d_scores, plain_split_heads(k), preferred_element_type=jnp.float32
    ) * HEAD_DIM ** (-0.5)
    d_key = jnp.einsum(
        "hqk,qhd->khd", d_scores, plain_split_heads(q), preferred_element_type=jnp.float32
    ) * HEAD_DIM ** (-0.5)
    rows_query = q.shape[0]
    rows_key = k.shape[0]
    return (
        d_query.reshape(rows_query, -1),
        d_key.reshape(rows_key, -1),
        d_value.reshape(rows_key, -1),
    )


def plain_attention_forward(h, norm_gain, w_qkv, w_out, key_mask):
    normed, inv_root = plain_norm_forward(h, norm_gain)
    normed_low = normed.astype(jnp.bfloat16)
    joined = plain_product(normed_low, w_qkv).astype(jnp.bfloat16)
    q, k, v = jnp.split(joined, 3, axis=1)
    output, log_total = plain_attend_forward(q, k, v, key_mask)
    output_low = output.astype(jnp.bfloat16)
    return (normed_low, inv_root, joined, output_low, log_total, plain_product(output_low, w_out))


def plain_attention_back(d_h, h, saved, norm_gain, w_qkv, w_out, key_mask):
    normed_low, inv_root, joined, output_low, log_total, unused = saved
    d_low = d_h.astype(jnp.bfloat16)
    d_wout = plain_product(output_low.T, d_low)
    d_output = plain_product(d_low, w_out.T).astype(jnp.bfloat16)
    q, k, v = jnp.split(joined, 3, axis=1)
    d_query, d_key, d_value = plain_attend_back(q, k, v, key_mask, log_total, d_output)
    d_joined = jnp.concatenate([d_query, d_key, d_value], axis=1).astype(jnp.bfloat16)
    d_wqkv = plain_product(normed_low.T, d_joined)
    d_normed = plain_product(d_joined, w_qkv.T)
    d_input, d_gain = plain_norm_back(d_normed, h, inv_root, norm_gain)
    return (d_input, d_gain, d_wqkv, d_wout)


def plain_mlp_forward(h, norm_gain, w_in, w_down):
    normed, inv_root = plain_norm_forward(h, norm_gain)
    normed_low = normed.astype(jnp.bfloat16)
    joined = plain_product(normed_low, w_in)
    gate, upper = jnp.split(joined, 2, axis=1)
    hidden_low = (jax.nn.gelu(gate, approximate=True) * upper).astype(jnp.bfloat16)
    return (normed_low, inv_root, joined, hidden_low, plain_product(hidden_low, w_down))


def plain_mlp_back(d_h, h, saved, norm_gain, w_in, w_down):
    normed_low, inv_root, joined, hidden_low, unused = saved
    d_low = d_h.astype(jnp.bfloat16)
    d_wdown = plain_product(hidden_low.T, d_low)
    d_hidden = plain_product(d_low, w_down.T)
    gate, upper = jnp.split(joined, 2, axis=1)
    active, active_back = jax.vjp(partial(jax.nn.gelu, approximate=True), gate)
    d_gate = active_back(d_hidden * upper)[0]
    d_upper = d_hidden * active
    d_joined = jnp.concatenate([d_gate, d_upper], axis=1).astype(jnp.bfloat16)
    d_win = plain_product(normed_low.T, d_joined)
    d_normed = plain_product(d_joined, w_in.T)
    d_input, d_gain = plain_norm_back(d_normed, h, inv_root, norm_gain)
    return (d_input, d_gain, d_win, d_wdown)


def encoder_forward(weights, source):
    gains, w_qkv, w_out, w_cross, w_in, w_down = weights
    inputs = source.astype(jnp.float32)
    attn_saved = plain_attention_forward(inputs, gains[0], w_qkv, w_out, None)
    middle = inputs + attn_saved[-1]
    mlp_saved = plain_mlp_forward(middle, gains[1], w_in, w_down)
    final = middle + mlp_saved[-1]
    normed, inv_root = plain_norm_forward(final, gains[2])
    memory = normed.astype(jnp.bfloat16)
    key_value = plain_product(memory, w_cross).astype(jnp.bfloat16)
    return (inputs, attn_saved, middle, mlp_saved, final, inv_root, memory, key_value)


def encoder_front(weights, source):
    saved = encoder_forward(weights, source)
    return (saved[7], saved[6])


def encoder_back_saved(weights, saved, d_keyvalue):
    gains, w_qkv, w_out, w_cross, w_in, w_down = weights
    inputs, attn_saved, middle, mlp_saved, final, inv_root, memory, key_value = saved
    d_wcross = plain_product(memory.T, d_keyvalue)
    d_memory = plain_product(d_keyvalue, w_cross.T)
    d_final, gain_last = plain_norm_back(d_memory, final, inv_root, gains[2])
    d_part, gain_mlp, d_win, d_wdown = plain_mlp_back(d_final, middle, mlp_saved, gains[1], w_in, w_down)
    d_middle = d_final + d_part
    d_first, gain_attn, d_wqkv, d_wout = plain_attention_back(
        d_middle, inputs, attn_saved, gains[0], w_qkv, w_out, None
    )
    grads = (jnp.stack([gain_attn, gain_mlp, gain_last]), d_wqkv, d_wout, d_wcross, d_win, d_wdown)
    return (d_middle + d_first, grads)


def encoder_back(weights, source, d_keyvalue):
    return encoder_back_saved(weights, encoder_forward(weights, source), d_keyvalue)


def decoder_pass(weights, source, key_value, weight_cot, length, factor):
    gains, w_qkv, w_out, w_cross, w_in, w_down = weights
    width = source.shape[1]
    inputs = source.astype(jnp.float32)
    position = jnp.arange(inputs.shape[0], dtype=jnp.int32)
    is_valid = position < length
    key_mask = (position[None, :] <= position[:, None]) & is_valid[None, :]
    attn_saved = plain_attention_forward(inputs, gains[0], w_qkv, w_out, key_mask)
    middle = inputs + attn_saved[-1]
    normed, inv_root = plain_norm_forward(middle, gains[1])
    normed_low = normed.astype(jnp.bfloat16)
    w_query = w_cross[:, :width]
    w_back = w_cross[:, width:]
    queries = plain_product(normed_low, w_query).astype(jnp.bfloat16)
    mem_keys = key_value[:, :width]
    mem_values = key_value[:, width:]
    cross_out, cross_total = plain_attend_forward(queries, mem_keys, mem_values, None)
    cross_low = cross_out.astype(jnp.bfloat16)
    after = middle + plain_product(cross_low, w_back)
    mlp_saved = plain_mlp_forward(after, gains[2], w_in, w_down)
    final = after + mlp_saved[-1]
    d_final = jnp.where(is_valid[:, None], weight_cot.astype(jnp.float32) * factor, 0.0)
    d_part, gain_mlp, d_win, d_wdown = plain_mlp_back(d_final, after, mlp_saved, gains[2], w_in, w_down)
    d_after = d_final + d_part
    d_low = d_after.astype(jnp.bfloat16)
    d_wback = plain_product(cross_low.T, d_low)
    d_cross = plain_product(d_low, w_back.T).astype(jnp.bfloat16)
    d_query, d_key, d_value = plain_attend_back(queries, mem_keys, mem_values, None, cross_total, d_cross)
    d_query_low = d_query.astype(jnp.bfloat16)
    d_wquery = plain_product(normed_low.T, d_query_low)
    d_normed = plain_product(d_query_low, w_query.T)
    d_norm_in, gain_cross = plain_norm_back(d_normed, middle, inv_root, gains[1])
    d_middle = d_after + d_norm_in
    d_keyvalue = jnp.concatenate([d_key, d_value], axis=1).astype(jnp.bfloat16)
    d_first, gain_attn, d_wqkv, d_wout = plain_attention_back(
        d_middle, inputs, attn_saved, gains[0], w_qkv, w_out, key_mask
    )
    grads = (
        jnp.stack([gain_attn, gain_cross, gain_mlp]),
        d_wqkv,
        d_wout,
        jnp.concatenate([d_wquery, d_wback], axis=1),
        d_win,
        d_wdown,
    )
    return (final.astype(jnp.bfloat16), d_middle + d_first, d_keyvalue, grads)


def on_section(flag, work, operands):

    def run_work(values):
        return work(*values)

    def skip_work(values):
        return jax.tree.map(jnp.zeros_like, work(*values))

    return lax.cond(flag, run_work, skip_work, operands)


def plain_body(
    block_in,
    cotangent,
    lengths,
    sources,
    loss_weight,
    gains,
    qkv_weight,
    out_weight,
    cross_weight,
    in_weight,
    down_weight,
):
    is_encoder = lax.axis_index("section") == 0
    is_decoder = jnp.logical_not(is_encoder)
    wide = lax.axis_size("dp")
    gathered = (
        lax.all_gather(gains, "dp", axis=2, tiled=True),
        lax.all_gather(qkv_weight, "dp", axis=1, tiled=True),
        lax.all_gather(out_weight, "dp", axis=1, tiled=True),
        lax.all_gather(cross_weight, "dp", axis=1, tiled=True),
        lax.all_gather(in_weight, "dp", axis=1, tiled=True),
        lax.all_gather(down_weight, "dp", axis=1, tiled=True),
    )
    weights = tuple((w[0] for w in gathered))
    onehot = (sources[:, None] == jnp.arange(3, dtype=jnp.int32)[None, :]).astype(jnp.float32)
    counts = lax.psum(jnp.sum(onehot * lengths[:, None].astype(jnp.float32), axis=0), "dp")
    own_count = jnp.sum(onehot * counts[None, :], axis=1)
    own_weight = jnp.sum(onehot * loss_weight[None, :].astype(jnp.float32), axis=1)
    scale = own_weight * (lengths.shape[0] * wide * block_in.shape[2] / 3.0) / own_count

    def step(carry, item):
        source, weight_cot, length, factor = item
        key_value, memory = on_section(is_encoder, encoder_front, (weights, source))
        received = shifted(key_value, "section", 1)
        decoded, table_grad, d_keyvalue, dec_grads = on_section(
            is_decoder, decoder_pass, (weights, source, received, weight_cot, length, factor)
        )
        returned = shifted(d_keyvalue, "section", -1)
        plot_grad, enc_grads = on_section(is_encoder, encoder_back, (weights, source, returned))
        grads = tuple((a + b for a, b in zip(dec_grads, enc_grads)))
        carry = tuple((a + b for a, b in zip(carry, grads)))
        return (carry, (memory + decoded, plot_grad + table_grad))

    start = tuple((jnp.zeros(w.shape, jnp.float32) for w in weights))
    carry, (outputs, input_grads) = lax.scan(step, start, (block_in[0], cotangent, lengths, scale))
    gain_total, qkv_total, out_total, cross_sum, in_total, down_total = carry
    reduced = (
        lax.psum_scatter(gain_total[None], "dp", scatter_dimension=2, tiled=True),
        lax.psum_scatter(qkv_total[None], "dp", scatter_dimension=1, tiled=True),
        lax.psum_scatter(out_total[None], "dp", scatter_dimension=1, tiled=True),
        lax.psum_scatter(cross_sum[None], "dp", scatter_dimension=1, tiled=True),
        lax.psum_scatter(in_total[None], "dp", scatter_dimension=1, tiled=True),
        lax.psum_scatter(down_total[None], "dp", scatter_dimension=1, tiled=True),
    )
    return (
        outputs[None],
        input_grads[None],
        reduced[0],
        reduced[1],
        reduced[2],
        reduced[3],
        reduced[4],
        reduced[5],
    )


def pad_block(block, rows, columns):
    return jnp.pad(block, ((0, rows - block.shape[0]), (0, columns - block.shape[1])))


def tiled_body(
    block_in, cotangent, lengths, sources, loss_weight, gains, qkv_weight, out_weight, cross_weight, in_weight, down_weight
):
    wide = lax.axis_size("dp")
    pairs, seq, width = block_in.shape[1:]
    own = gains.shape[2]
    onehot = (sources[:, None] == jnp.arange(3, dtype=jnp.int32)[None, :]).astype(jnp.float32)
    counted = jnp.sum(onehot * lengths[:, None].astype(jnp.float32), axis=0, keepdims=True)
    gains_wide, counts_wide, w_qkv, w_out, w_enc, w_dec, w_in, w_down = gather_weights(
        wide,
        pad_block(gains[0], 16, 128),
        pad_block(counted, 8, 128),
        qkv_weight[0],
        out_weight[0],
        cross_weight[0],
        in_weight[0],
        down_weight[0],
    )
    counts = jnp.sum(counts_wide.reshape(wide, 8, 128)[:, 0, :3], axis=0)
    gains_full = gains_wide.reshape(wide, 16, 128)[:, :8, :own].transpose(1, 0, 2).reshape(8, width).astype(jnp.float32)
    own_count = jnp.sum(onehot * counts[None, :], axis=1)
    own_weight = jnp.sum(onehot * loss_weight[None, :].astype(jnp.float32), axis=1)
    scale = own_weight * (pairs * wide * seq / 3.0) / own_count

    x = block_in.reshape(pairs * seq, width)
    *saved, landed = forward(x, lengths, gains_full, w_qkv, w_out, w_in, w_down, seq)
    block_out, input_grad, gains_part, g_down, g_in, g_dec, g_enc, g_out, g_qkv, _ = backward(
        seq, lengths, scale, x, gains_full, cotangent.reshape(pairs * seq, width), saved, landed,
        (w_qkv, w_out, w_enc, w_dec, w_in, w_down),
    )
    g_gains = gains_part.reshape(8, wide, own).transpose(1, 0, 2)
    g_gains = jnp.pad(g_gains, ((0, 0), (0, 0), (0, 128 - own))).reshape(wide * 8, 128)
    down, inner, cross, out, qkv, gains_sum = reduce_grads(
        wide,
        {"down": g_down, "in": g_in, "crossD": g_dec, "crossE": g_enc, "out": g_out, "qkv": g_qkv, "gains": g_gains},
    )
    return (
        block_out.reshape(block_in.shape),
        input_grad.reshape(block_in.shape),
        gains_sum[None, :3, :own],
        qkv[None],
        out[None],
        cross[None],
        inner[None],
        down[None],
    )


def solution(mesh):
    in_specs = (
        P("section", "dp", None, None),
        P("dp", None, None),
        P("dp"),
        P("dp"),
        P(),
        P("section", None, "dp"),
        P("section", "dp", None),
        P("section", "dp", None),
        P("section", "dp", None),
        P("section", "dp", None),
        P("section", "dp", None),
    )
    out_specs = (
        P("section", "dp", None, None),
        P("section", "dp", None, None),
        P("section", None, "dp"),
        P("section", "dp", None),
        P("section", "dp", None),
        P("section", "dp", None),
        P("section", "dp", None),
        P("section", "dp", None),
    )

    def body(*args):
        shards = args[6:]
        tiled = args[5].shape[2] <= 128 and all(w.shape[1] % 16 == 0 for w in shards)
        return (tiled_body if tiled else plain_body)(*args)

    return jax.shard_map(body, mesh=mesh, in_specs=in_specs, out_specs=out_specs, check_vma=False)
```

time: 1330 us -> 406 us (0.31)
  waiting for transfers between devices: 924 us -> 0 us
  Pallas kernels: 0 us -> 380 us
  other arithmetic: 126 us -> 4.33 us
  matrix products: 112 us -> 0 us
  local copies, waits for them, and re-layouts: 79.1 us -> 12 us
  blocking collectives: 53.5 us -> 0 us
    reduce_scatter x5 -> x0, waiting for transfers between devices: 467 us -> none  [the longest x1 140 us: body(): lax.psum_scatter(in_total[None], 'dp', scatter_dimension=1, tiled=True)]
    pallas_call x0 -> x4, Pallas kernels: none -> 380 us  [the longest x1 139 us: backward(): pl.pallas_call(partial(backward_kernel, seq), out_shape=[shaped((rows, wi...]
    ppermute x4 -> x0, waiting for transfers between devices: 216 us -> none  [shifted(): return lax.ppermute(block, axis, route)]
    all_gather x5 -> x0, waiting for transfers between devices: 184 us -> none  [the longest x1 63 us: body(): lax.all_gather(in_weight, 'dp', axis=1, tiled=True)]
    add x18 -> x0, other arithmetic: 104 us -> none  [the longest x12 100 us: step(): carry = tuple((a + b for a, b in zip(carry, grads)))]
    dot_general x52 -> x0, matrix products: 104 us -> none  [the longest x38 86.4 us: product(): return jnp.dot(a, b, preferred_element_type=jnp.float32)]
    unnamed x12 -> x0, waiting for transfers between devices: 56.4 us -> none
    another operation x24 -> x0, local copies, waits for them, and re-layouts: 42.3 us -> none
  transfers between devices with their start and end apart: 15 -> 0, of which waited for: 14 -> 0; matrix products, arithmetic and copies ran while one was open for 1% -> 0% of each run, Pallas kernels for 0% -> 0%
where the time goes in v2:
time: 406 us; the launch traced here: 398 us
  Pallas kernels  380 us (94%)
  local copies, waits for them, and re-layouts  12 us (3%)
  other arithmetic  4.33 us (1%)
    pallas_call x1, Pallas kernels, backward(): pl.pallas_call(partial(backward_kernel, seq), out_shape=[shaped((rows, wi...  139 us
    pallas_call x1, Pallas kernels, reduce_grads(): pl.pallas_call(partial(reduce_kernel, wide), out_shape=[jax.ShapeDtypeStr...  95.6 us
    pallas_call x1, Pallas kernels, gather_weights(): pl.pallas_call(partial(gather_kernel, wide), out_shape=[jax.ShapeDtypeStr...  77.4 us
    pallas_call x1, Pallas kernels, forward(): pl.pallas_call(partial(forward_kernel, seq), out_shape=[jax.ShapeDtypeStr...  68.4 us

profile of v2, /device:TPU:0, one launch (start us, length us, event | category | flops | bytes accessed | tf_op | source)
XLA Modules:
  0.0 397.7 jit_solution(16585758036293537761)
XLA Ops:
  0.6 0.7 convert_element_type.22
  1.3 0.7 convert_element_type.23
  1.9 0.7 select_reduce_fusion.1
  2.7 0.6 pad.13.refs_1_
  3.3 1.3 pad.12.refs_0_
  4.6 77.4 %gather_weights.1 = (bf16[256,128]{1,0:T(8,128)(2,1)}, f32[128,128]{1,0:T(8,128)}, bf16[768,2304]{1,0:T(8,128)(2,1)}, bf16[768,768]{1,0:T(8,128)(2,1)}, bf16[768...) custom-call(bf16[16,128]{1,0:T(8,128)(2,1)} %pad.12.refs_0_, ...), custom_call_target="tpu_custom_call" | custom-call | tf_op jit(solution)/shard_map/gather_weights/pallas_call | solution.py:215
  81.9 0.9 slice_reduce_fusion
  82.8 0.8 slice.13
  83.6 0.9 select_reduce_fusion.2
  84.4 0.5 multiply_divide_fusion.factors
  85.0 0.7 reshape.57.gains_in
  85.7 68.4 %forward.1 = (bf16[512,2304]{1,0:T(8,128)(2,1)}, bf16[512,768]{1,0:T(8,128)(2,1)}, f32[512,768]{1,0:T(8,128)}, f32[512,768]{1,0:T(8,128)}, bf16[512,768]{1,0:T(8,128)(2,1)}, /*index=5*/bf16[512,768]{1,0:T(8,128)(2,1)}) custom-call(s32[2]{0:T(128)} %lengths.3, bf16[512,768]{1,0:T(8,128)(2,1)} %bitcast.27, f32[8,768]{1,0:T(8,128)} %reshape.57.gains_in, ...), custom_call_target="tpu_custom_call" | custom-call | tf_op jit(solution)/shard_map/forward/pallas_call | solution.py:656
  154.0 139.1 %backward.1 = (bf16[512,768]{1,0:T(8,128)(2,1)}, f32[512,768]{1,0:T(8,128)}, f32[8,768]{1,0:T(8,128)}, bf16[2048,768]{1,0:T(8,128)(2,1)}, bf16[768,4096]{1,0:T(8...) custom-call(s32[2]{0:T(128)} %lengths.3, ...), custom_call_target="tpu_custom_call" | custom-call | tf_op jit(solution)/shard_map/backward/pallas_call | solution.py:885
  293.2 0.8 reshape.55
  294.0 0.6 pad_bitcast_fusion.refs_6_
  294.7 0.0 copy-start.1
  294.7 95.6 %reduce_grads.1 = (f32[128,768]{1,0:T(8,128)}, f32[48,4096]{1,0:T(8,128)}, f32[48,1536]{1,0:T(8,128)}, f32[48,768]{1,0:T(8,128)}, f32[48,2304]{1,0:T(8,128)}, /*index=5*/f32[8,128]{1,0:T(8,128)}) custom-call(bf16[2048,768]{1,0:T(8,128)(2,1)} %get-tuple-element.53.refs_0_, bf16[768,4096]{1,0:T(8,128)(2,1)} %get-tuple-element.54.refs_1_, ...), custom_call_target="tpu_custom_call" | custom-call | tf_op jit(solution)/shard_map/reduce_grads/pallas_call | solution.py:384
  390.3 0.0 copy-start
  390.3 0.8 slice_bitcast_fusion
  391.1 0.6 copy.24
  391.6 0.0 copy-done.1
  391.6 0.0 copy-start.3
  391.6 0.9 copy.36
  392.5 0.0 copy-done
  392.5 0.0 copy-start.6
  392.5 0.0 copy-start.5
  392.5 0.0 copy-start.2
  392.5 1.1 copy.37
  393.7 0.0 copy-done.3
  393.7 0.0 copy-start.4
  393.7 0.8 copy.38
  394.5 0.0 copy-done.6
  394.5 0.7 copy.39
  395.1 0.0 copy-done.5
  395.1 0.7 copy.40
  395.8 0.0 copy-done.2
  395.8 0.9 copy.41
  396.7 0.0 copy-done.4
  396.7 0.7 copy.42
  (2 shorter events, 0.0 us)
Async XLA Ops:
  294.7 97.0 %copy-start.1 = (bf16[512,768]{1,0:T(8,128)(2,1)S(1)}, bf16[512,768]{1,0:T(8,128)(2,1)}, u32[]{:S(2)}) copy-start(bf16[512,768]{1,0:T(8,128)(2,1)} %get-tuple-element.51) | copy-start | bytes 2359300
  390.3 2.3 copy-start
  391.6 2.0 copy-start.3
  392.5 1.9 copy-start.6
  392.5 2.6 copy-start.5
  392.5 3.3 copy-start.2
  393.7 3.0 copy-start.4
